TPU v7x, 128 devices: a whole 4x4x4 slice. The times are simulated.
128 devices in a mesh: frame: 16 (over y, x_lo, core), row: 4 (over z), col: 2 (over x_hi).
Axes of the slice: x: 4 (x_hi: 2, x_lo: 2; x = x_hi * 2 + x_lo), y: 4, z: 4, core: 2. Of those that a mesh axis runs over, the one named last changes fastest.
Arguments:
- images: bfloat16 [64, 8, 4, 2, 128, 128], P('frame', 'row', 'col'), may hold values from -36 to 36
- corners: int32 [2, 64, 8, 4], P(None, 'frame', 'row', 'col'), may hold values from -16 to 16
- window_kind_index: int32 [8, 4], P('row', 'col'), may hold values from 0 to 3
- coefficients: float32 [64, 8, 4, 36], P('frame', 'row', 'col'), may hold values from -2.5 to 2.5
- step_size: float32 [], replicated, may hold values from 0.1 to 0.4
- noise_weight: float32 [], replicated, may hold values from 0.5 to 4
- smooth_weight: float32 [], replicated, may hold values from 0.3 to 3
Outputs:
- coefficients_out: float32 [64, 8, 4, 36], P('frame', 'row', 'col')
- object_spectrum: float32 [2, 8, 4, 128, 128], P(None, 'row', 'col', 'frame')
All inputs are finite; a program needn't handle non-finite values.
Results may differ from a plain program's by a relative error of at most 0.0003.
Values sent between devices are 32-bit elements; how exact they have to be, the bound alone decides.
A program may use at most 128 MiB of HBM per device.

v0:
```python
import math

import jax
import jax.numpy as jnp
from jax import lax
from jax.sharding import PartitionSpec as P

WINDOW_KINDS = 4
ITERS = 2


DIVERSITY = 1.5
TINY = 1e-06
EXACT = lax.Precision.HIGHEST


def padded_2(cells, sides, width):
    for axis, dim in sides:
        count = lax.axis_size(axis)
        ends = count - 1
        head = lax.slice_in_dim(cells, 0, width, axis=dim)
        tail = lax.slice_in_dim(cells, cells.shape[dim] - width, cells.shape[dim], axis=dim)
        cells = jnp.concatenate(
            [
                lax.ppermute(tail, axis, [(i, (i + 1) % count) for i in range(ends)]),
                cells,
                lax.ppermute(head, axis, [((i + 1) % count, i) for i in range(ends)]),
            ],
            axis=dim,
        )
    return cells


def noll_order(mode_index):
    radial_order = (math.isqrt(8 * (mode_index - 1) + 1) - 1) // 2
    position = mode_index - radial_order * (radial_order + 1) // 2
    parity = radial_order % 2
    azimuth = (position + parity) // 2 * 2 - parity
    if azimuth != 0 and mode_index % 2 == 1:
        azimuth = -azimuth
    return (radial_order, azimuth)


def radial_poly(radial_order, azimuth, radius):
    summed = jnp.zeros(radius.shape, jnp.float32)
    for term_index in range((radial_order - azimuth) // 2 + 1):
        factor = (
            (-1) ** term_index
            * math.factorial(radial_order - term_index)
            / (
                math.factorial(term_index)
                * math.factorial((radial_order + azimuth) // 2 - term_index)
                * math.factorial((radial_order - azimuth) // 2 - term_index)
            )
        )
        summed = summed + factor * radius ** (radial_order - 2 * term_index)
    return summed


def zernike_table(pixels, modes):
    offsets = (jnp.arange(pixels, dtype=jnp.float32) - pixels / 2.0) / (pixels // 4)
    ones_line = jnp.ones((pixels,), jnp.float32)
    rows_grid = offsets[:, None] * ones_line[None, :]
    cols_grid = ones_line[:, None] * offsets[None, :]
    radius = jnp.sqrt(rows_grid * rows_grid + cols_grid * cols_grid)
    azimuth_angle = jnp.arctan2(rows_grid, cols_grid)
    pupil_mask = jnp.where(radius <= 1.0, 1.0, 0.0).astype(jnp.float32)
    shapes = []
    for mode_index in range(2, modes + 2):
        radial_order, azimuth = noll_order(mode_index)
        radial = radial_poly(radial_order, abs(azimuth), radius)
        if azimuth == 0:
            mode_shape = math.sqrt(radial_order + 1) * radial
        elif azimuth > 0:
            mode_shape = (
                math.sqrt(2 * (radial_order + 1)) * radial * jnp.cos(azimuth * azimuth_angle)
            )
        else:
            mode_shape = (
                math.sqrt(2 * (radial_order + 1)) * radial * jnp.sin(-azimuth * azimuth_angle)
            )
        shapes.append(mode_shape * pupil_mask)
    return (jnp.stack(shapes), pupil_mask)


def dft_tables(pixels):
    indices = jnp.arange(pixels, dtype=jnp.int32)
    product = indices[:, None] * indices[None, :] % pixels
    angles = product.astype(jnp.float32) * (2.0 * math.pi / pixels)
    return (jnp.cos(angles), -jnp.sin(angles))


def transform(real_part, imag_part, cosine, sine):
    if imag_part is None:
        half_real = jnp.matmul(real_part, cosine, precision=EXACT)
        half_imag = jnp.matmul(real_part, sine, precision=EXACT)
    else:
        half_real = jnp.matmul(real_part, cosine, precision=EXACT) - jnp.matmul(
            imag_part, sine, precision=EXACT
        )
        half_imag = jnp.matmul(real_part, sine, precision=EXACT) + jnp.matmul(
            imag_part, cosine, precision=EXACT
        )
    out_real = jnp.einsum("uy,...yx->...ux", cosine, half_real, precision=EXACT) - jnp.einsum(
        "uy,...yx->...ux", sine, half_imag, precision=EXACT
    )
    out_imag = jnp.einsum("uy,...yx->...ux", sine, half_real, precision=EXACT) + jnp.einsum(
        "uy,...yx->...ux", cosine, half_imag, precision=EXACT
    )
    return (out_real, out_imag)


def window_table(pixels, kinds):
    positions = jnp.arange(pixels, dtype=jnp.int32)
    edges = jnp.minimum(positions, pixels - 1 - positions).astype(jnp.float32)
    widths = ((jnp.arange(kinds, dtype=jnp.int32) + 1) * pixels // 16).astype(jnp.float32)
    taper = jnp.where(
        edges[None, :] < widths[:, None],
        0.5 - 0.5 * jnp.cos(math.pi * (edges[None, :] + 0.5) / widths[:, None]),
        1.0,
    )
    return taper[:, :, None] * taper[:, None, :]


def spectra(images, corners, window_kind_index, cosine, sine, kinds):
    pixels = images.shape[-1]
    tables = window_table(pixels, kinds)
    choose = (window_kind_index[..., None] == jnp.arange(kinds, dtype=jnp.int32)).astype(
        jnp.float32
    )
    window = jnp.einsum("rck,kyx->rcyx", choose, tables, precision=EXACT)
    windowed = images.astype(jnp.float32) * window[None, :, :, None]
    part_real, part_imag = transform(windowed, None, cosine, sine)
    frequency = jnp.arange(pixels, dtype=jnp.int32)
    shift_rows = corners[0][:, :, :, None, None, None]
    shift_cols = corners[1][:, :, :, None, None, None]
    phase_index = (
        frequency[:, None] * shift_rows % pixels + frequency[None, :] * shift_cols % pixels
    ) % pixels
    angles = phase_index.astype(jnp.float32) * (2.0 * math.pi / pixels)
    ramp_real = jnp.cos(angles) / pixels
    ramp_imag = jnp.sin(angles) / pixels
    return (
        part_real * ramp_real - part_imag * ramp_imag,
        part_real * ramp_imag + part_imag * ramp_real,
    )


def optics(values, basis, pupil_mask, cosine, sine):
    pixels = basis.shape[-1]
    flat_phase = jnp.matmul(values, basis.reshape(basis.shape[0], pixels * pixels), precision=EXACT)
    phases = flat_phase.reshape(values.shape[:-1] + (1, pixels, pixels))
    diverse = jnp.stack([jnp.zeros_like(basis[2]), DIVERSITY * basis[2]])
    phases = phases + diverse
    field_real = pupil_mask * jnp.cos(phases)
    field_imag = pupil_mask * jnp.sin(phases)
    spot_real, spot_imag = transform(field_real, field_imag, cosine, sine)
    spread = spot_real * spot_real + spot_imag * spot_imag
    spread = spread / jnp.sum(spread, axis=(-2, -1), keepdims=True)
    return transform(spread, None, cosine, sine)


def body(images, corners, window_kind_index, coefficients, step_size, noise_weight, smooth_weight):
    pixels = images.shape[-1]
    cosine, sine = dft_tables(pixels)
    basis, pupil_mask = zernike_table(pixels, coefficients.shape[-1])
    data_real, data_imag = spectra(images, corners, window_kind_index, cosine, sine, WINDOW_KINDS)
    count_all = (
        coefficients.size * lax.axis_size("frame") * lax.axis_size("row") * lax.axis_size("col")
    )

    def local_optics(values):
        return optics(values, basis, pupil_mask, cosine, sine)

    object_real = None
    object_imag = None
    for iteration in range(ITERS):
        padded = padded_2(coefficients, (("row", 1), ("col", 2)), 1)
        (otf_real, otf_imag), pullback = jax.vjp(local_optics, coefficients)
        local_real = jnp.sum(otf_real * data_real + otf_imag * data_imag, axis=(0, 3))
        local_imag = jnp.sum(otf_real * data_imag - otf_imag * data_real, axis=(0, 3))
        local_power = jnp.sum(otf_real * otf_real + otf_imag * otf_imag, axis=(0, 3))
        cross_real, cross_imag, power_sum = (
            lax.psum_scatter(local_real, "frame", scatter_dimension=2, tiled=True),
            lax.psum_scatter(local_imag, "frame", scatter_dimension=2, tiled=True),
            lax.psum_scatter(local_power, "frame", scatter_dimension=2, tiled=True),
        )
        object_real = cross_real / (power_sum + noise_weight)
        object_imag = cross_imag / (power_sum + noise_weight)
        whole_real, whole_imag = (
            lax.all_gather(object_real, "frame", axis=2, tiled=True),
            lax.all_gather(object_imag, "frame", axis=2, tiled=True),
        )
        full_real = whole_real[None, :, :, None]
        full_imag = whole_imag[None, :, :, None]
        res_real = data_real - (full_real * otf_real - full_imag * otf_imag)
        res_imag = data_imag - (full_real * otf_imag + full_imag * otf_real)
        cot_real = -2.0 * (res_real * full_real + res_imag * full_imag)
        cot_imag = 2.0 * (res_real * full_imag - res_imag * full_real)
        grads = pullback((cot_real, cot_imag))[0]
        total = lax.psum(jnp.sum(grads * grads), ("frame", "row", "col"))
        scale = jnp.sqrt(total / count_all + TINY)
        laplace = (
            4.0 * coefficients
            - padded[:, 2:, 1:-1]
            - padded[:, :-2, 1:-1]
            - padded[:, 1:-1, 2:]
            - padded[:, 1:-1, :-2]
        )
        coefficients = coefficients - step_size * (grads / scale + smooth_weight * laplace)
    return (coefficients, jnp.stack([object_real, object_imag]))


def solution(mesh):
    in_specs = (
        P("frame", "row", "col", None, None, None),
        P(None, "frame", "row", "col"),
        P("row", "col"),
        P("frame", "row", "col", None),
        P(),
        P(),
        P(),
    )
    out_specs = (P("frame", "row", "col", None), P(None, "row", "col", "frame", None))
    return jax.shard_map(body, mesh=mesh, in_specs=in_specs, out_specs=out_specs, check_vma=False)
```

profile of v0, /device:TPU:1, one launch (start us, length us, event | category | flops | bytes accessed | tf_op | source)
XLA Modules:
  0.0 858.3 jit_solution(12371175773242543064)
XLA Ops:
  35.1 7.7 multiply_multiply_fusion.21
  42.7 11.0 %multiply_multiply_fusion.36 = (f32[1,16384]{1,0:T(1,128)S(1)}, f32[1,16384]{1,0:T(1,128)S(1)}, f32[1,16384]{1,0:T(1,128)S(1)}, f32[1,16384]{1,0:T(1,128)S(1)}, ...) fusion(f32[1,16384]{1,0:T(1,128)S(1)} %get-tuple-element.99, ...), kind=kLoop, calls=%fused_computation.496 | loop fusion | flops 1802240 | bytes 2097152 | tf_op jit(solution)/shard_map/mul | solution.py:82
  53.9 7.4 stack.12
  92.9 8.7 %fusion.18 = f32[4,2,2,2,128,128]{5,4,3,2,1,0:T(8,128)S(1)} fusion(f32[2,128,128]{2,1,0:T(8,128)S(1)} %stack.13, f32[128,128]{1,0:T(8,128)S(1)} %fusion.317, f32[4,2,2,128,128]{4,3,0,2,1:T(8,128)S(1)} %add.1537), kind=kOutput, calls=%fused_computation.18 | convolution fusion | flops 806600704 | bytes 3342336 | tf_op jit(solution)/shard_map/jvp()/dot_general | solution.py:98
  101.7 8.8 %fusion.93 = f32[4,2,2,2,128,128]{5,4,3,2,1,0:T(8,128)S(1)} fusion(f32[4,2,2,2,128,128]{5,4,3,2,1,0:T(8,128)S(1)} %fusion.18, f32[2,128,128]{2,1,0:T(8,128)S(1)} %stack.13, f32[128,128]{1,0:T(8,128)S(1)} %fusion.317, f32[4,2,2,128,128]{4,3,0,2,1:T(8,128)S(1)} %add.1537), kind=kOutput, calls=%fused_computation.136 | convolution fusion | flops 807108608 | bytes 5439488 | tf_op jit(solution)/shard_map/jvp()/dot_general | solution.py:98
  118.2 8.7 %fusion.16 = f32[4,2,2,2,128,128]{5,4,3,2,1,0:T(8,128)S(1)} fusion(f32[2,128,128]{2,1,0:T(8,128)S(1)} %stack.13, f32[128,128]{1,0:T(8,128)S(1)} %fusion.317, f32[4,2,2,128,128]{4,3,0,2,1:T(8,128)S(1)} %add.1537), kind=kOutput, calls=%fused_computation.17 | convolution fusion | flops 806584320 | bytes 3342336 | tf_op jit(solution)/shard_map/jvp()/dot_general | solution.py:101
  126.9 8.8 %fusion.96 = f32[4,2,2,2,128,128]{5,4,3,2,1,0:T(8,128)S(1)} fusion(f32[4,2,2,2,128,128]{5,4,3,2,1,0:T(8,128)S(1)} %fusion.16, f32[2,128,128]{2,1,0:T(8,128)S(1)} %stack.13, f32[128,128]{1,0:T(8,128)S(1)} %fusion.317, f32[4,2,2,128,128]{4,3,0,2,1:T(8,128)S(1)} %add.1537), kind=kOutput, calls=%fused_computation.137 | convolution fusion | flops 807124992 | bytes 5439488 | tf_op jit(solution)/shard_map/jvp()/dot_general | solution.py:101
  166.2 10.8 %sine_multiply_fusion.1 = (f32[4,2,2,128,128]{4,3,2,1,0:T(8,128)}, f32[4,2,2,128,128]{4,3,2,1,0:T(8,128)}, f32[4,2,2,128,128]{4,3,2,1,0:T(8,128)}, f32[4,2,2,128,128]{4,3,2,1,0:T(8,128)}) fusion(s32[4,2,2,128]{3,2,1,0:T(2,128)S(1)} %get-tuple-element.128, s32[4,2,2,128]{3,2,1,0:T(2,128)S(1)} %get-tuple-element.129), kind=kLoop, calls=%fused_computation.174 | loop fusion | flops 8388608 | bytes 4210688 | tf_op jit(solution)/shard_map/div | solution.py:142
  186.7 8.2 fusion.65
  222.2 99.8 %all-reduce.14.cloned.1.call-done = (f32[2,2,128,128]{3,1,0,2:T(2,128)}, f32[2,2,128,128]{3,1,0,2:T(2,128)}, f32[2,2,128,128]{3,1,0,2:T(2,128)}) async-done(((f32[2,2,128,128]{3,1,0,2:T(2,128)}, f32[2,2,128,128]{3,1,0,2:T(2,128)}, f32[2,2,128,128]{3,1,0,2:T(2,128)}), (f32[2,2,128,128]{3,1,0,2:T(2,128)}, f32[2,2,128,128]{3,1,0,2:T(2,128)}, f32[2,2,128,128]{3,1,0,2:T(2,128)})) %all-reduce.14.cloned.1.call-update) | async-done | bytes 786448
  322.8 19.2 %all_gather.12 = f32[2,2,128,128]{3,1,0,2:T(2,128)} all-gather(f32[2,2,8,128]{3,1,0,2:T(2,128)S(1)} %get-tuple-element.44), channel_id=1, replica_groups=mesh['frame'=16,'row'=4,'col'=2] {'frame'}, dimensions={2}, use_global_device_ids=true | all-gather | bytes 278528 | tf_op jit(solution)/shard_map/all_gather | solution.py:191
  343.9 20.8 %all_gather.13 = f32[2,2,128,128]{3,1,0,2:T(2,128)} all-gather(f32[2,2,8,128]{3,1,0,2:T(2,128)S(1)} %get-tuple-element.45), channel_id=1, replica_groups=mesh['frame'=16,'row'=4,'col'=2] {'frame'}, dimensions={2}, use_global_device_ids=true | all-gather | bytes 278528 | tf_op jit(solution)/shard_map/all_gather | solution.py:192
  405.9 11.6 %fusion.34 = f32[4,2,2,128,128]{4,3,2,1,0:T(8,128)S(1)} fusion(f32[4,2,2,2,128,128]{5,4,3,2,1,0:T(8,128)S(1)} %fusion.56, f32[4,2,2,2,128,128]{5,4,3,2,1,0:T(8,128)S(1)} %fusion.53, f32[4,2,2,2,128,128]{5,4,3,2,1,0:T(8,128)S(1)} %fusion.55, f32[4,2,2,2,128,128]{5,4,3,2,1,0:T(8,128)S(1)} %fusion.105, f32[2,128,128]{2,1,0:T(8,128)S(1)} %stack.13, ...), kind=kOutput, calls=%fused_computation.32 | convolution fusion | flops 810516480 | bytes 10682368 | tf_op jit(solution)/shard_map/transpose(jvp())/dot_general | solution.py:101
  423.6 64.4 %psum.14 = f32[]{:T(128)} all-reduce(f32[]{:T(128)} %get-tuple-element.120), channel_id=1, replica_groups=mesh['frame'=16,'row'=4,'col'=2] {'frame','row','col'}, use_global_device_ids=true, to_apply=%region_10.11 | all-reduce | flops 1 | bytes 8 | tf_op jit(solution)/shard_map/psum | solution.py:201
  493.5 9.1 %fusion.10 = f32[4,2,2,2,128,128]{5,4,3,2,1,0:T(8,128)S(1)} fusion(f32[4,2,2,128,128]{4,3,2,1,0:T(8,128)S(1)} %copy.228, f32[2,128,128]{2,1,0:T(8,128)S(1)} %stack.13, f32[128,128]{1,0:T(8,128)S(1)} %fusion.317), kind=kOutput, calls=%fused_computation.14 | convolution fusion | flops 806600704 | bytes 3342336 | tf_op jit(solution)/shard_map/jvp()/dot_general | solution.py:98
  502.6 8.7 %fusion.99 = f32[4,2,2,2,128,128]{5,4,3,2,1,0:T(8,128)S(1)} fusion(f32[4,2,2,2,128,128]{5,4,3,2,1,0:T(8,128)S(1)} %fusion.10, f32[4,2,2,128,128]{4,3,2,1,0:T(8,128)S(1)} %copy.228, f32[2,128,128]{2,1,0:T(8,128)S(1)} %stack.13, f32[128,128]{1,0:T(8,128)S(1)} %fusion.317), kind=kOutput, calls=%fused_computation.138 | convolution fusion | flops 807108608 | bytes 5439488 | tf_op jit(solution)/shard_map/jvp()/dot_general | solution.py:98
  518.8 8.9 %fusion.8 = f32[4,2,2,2,128,128]{5,4,3,2,1,0:T(8,128)S(1)} fusion(f32[4,2,2,128,128]{4,3,2,1,0:T(8,128)S(1)} %copy.228, f32[2,128,128]{2,1,0:T(8,128)S(1)} %stack.13, f32[128,128]{1,0:T(8,128)S(1)} %fusion.317), kind=kOutput, calls=%fused_computation.13 | convolution fusion | flops 806584320 | bytes 3342336 | tf_op jit(solution)/shard_map/jvp()/dot_general | solution.py:101
  527.7 8.7 %fusion.102 = f32[4,2,2,2,128,128]{5,4,3,2,1,0:T(8,128)S(1)} fusion(f32[4,2,2,2,128,128]{5,4,3,2,1,0:T(8,128)S(1)} %fusion.8, f32[4,2,2,128,128]{4,3,2,1,0:T(8,128)S(1)} %copy.228, f32[2,128,128]{2,1,0:T(8,128)S(1)} %stack.13, f32[128,128]{1,0:T(8,128)S(1)} %fusion.317), kind=kOutput, calls=%fused_computation.139 | convolution fusion | flops 807124992 | bytes 5439488 | tf_op jit(solution)/shard_map/jvp()/dot_general | solution.py:101
  580.3 103.2 %all-reduce.12.cloned.1.call-done = (f32[2,2,128,128]{3,1,0,2:T(2,128)}, f32[2,2,128,128]{3,1,0,2:T(2,128)}, f32[2,2,128,128]{3,1,0,2:T(2,128)}) async-done(((f32[2,2,128,128]{3,1,0,2:T(2,128)}, f32[2,2,128,128]{3,1,0,2:T(2,128)}, f32[2,2,128,128]{3,1,0,2:T(2,128)}), (f32[2,2,128,128]{3,1,0,2:T(2,128)}, f32[2,2,128,128]{3,1,0,2:T(2,128)}, f32[2,2,128,128]{3,1,0,2:T(2,128)})) %all-reduce.12.cloned.1.call-update) | async-done | bytes 786448
  684.2 19.2 %all_gather.14 = f32[2,2,128,128]{3,1,0,2:T(2,128)} all-gather(f32[2,2,8,128]{3,1,0,2:T(2,128)S(1)} %get-tuple-element.42), channel_id=1, replica_groups=mesh['frame'=16,'row'=4,'col'=2] {'frame'}, dimensions={2}, use_global_device_ids=true | all-gather | bytes 278528 | tf_op jit(solution)/shard_map/all_gather | solution.py:191
  705.2 20.6 %all_gather.15 = f32[2,2,128,128]{3,1,0,2:T(2,128)} all-gather(f32[2,2,8,128]{3,1,0,2:T(2,128)S(1)} %get-tuple-element.43), channel_id=1, replica_groups=mesh['frame'=16,'row'=4,'col'=2] {'frame'}, dimensions={2}, use_global_device_ids=true | all-gather | bytes 278528 | tf_op jit(solution)/shard_map/all_gather | solution.py:192
  767.2 11.4 %fusion.32 = f32[4,2,2,128,128]{4,3,2,1,0:T(8,128)S(1)} fusion(f32[4,2,2,2,128,128]{5,4,3,2,1,0:T(8,128)S(1)} %fusion.38, f32[4,2,2,2,128,128]{5,4,3,2,1,0:T(8,128)S(1)} %fusion.35, f32[4,2,2,2,128,128]{5,4,3,2,1,0:T(8,128)S(1)} %fusion.37, f32[4,2,2,2,128,128]{5,4,3,2,1,0:T(8,128)S(1)} %fusion.108, f32[4,2,2,128,128]{4,3,2,1,0:T(8,128)S(1)} %copy.228, ...), kind=kOutput, calls=%fused_computation.30 | convolution fusion | flops 810516480 | bytes 10682368 | tf_op jit(solution)/shard_map/transpose(jvp())/dot_general | solution.py:101
  778.6 6.1 multiply_reduce_fusion
  784.7 64.4 %psum.15 = f32[]{:T(128)} all-reduce(f32[]{:T(128)} %get-tuple-element.126), channel_id=1, replica_groups=mesh['frame'=16,'row'=4,'col'=2] {'frame','row','col'}, use_global_device_ids=true, to_apply=%region_21.22 | all-reduce | flops 1 | bytes 8 | tf_op jit(solution)/shard_map/psum | solution.py:201
  (231 shorter events, 282.6 us)
Async XLA Ops:
  7.2 8.7 %copy-start.23 = (bf16[4,2,2,2,128,128]{5,4,3,2,1,0:T(8,128)(2,1)S(1)}, bf16[4,2,2,2,128,128]{5,4,3,2,1,0:T(8,128)(2,1)}, u32[]{:S(2)}) copy-start(bf16[4,2,2,2,128,128]{5,4,3,2,1,0:T(8,128)(2,1)} %param.7) | copy-start | bytes 3145732
  7.2 314.9 %all-reduce.14.cloned.1.call-start = ((), (), s32[]{:S(2)}) async-start(), calls=%async_computation.1 | async-start | bytes 1572864
  8.0 207.4 %collective-permute-start = (f32[4,1,2,36]{3,0,2,1:T(4,128)S(1)}, f32[4,1,2,36]{3,0,2,1:T(4,128)S(1)}, u32[]{:S(2)}, u32[]{:S(2)}) collective-permute-start(f32[4,1,2,36]{3,0,2,1:T(4,128)S(1)} %get-tuple-element.110), channel_id=1, source_target_pairs={{2,0},{4,2},{6,4},{3,1},{5,3},{7,5},{10,8},{12,10},{14,12},{11,9},... | collective-permute-start | bytes 3464 | tf_op jit(solution)/shard_map/ppermute | solution.py:27
  9.3 206.1 %collective-permute-start.1 = (f32[4,1,2,36]{3,0,2,1:T(4,128)S(1)}, f32[4,1,2,36]{3,0,2,1:T(4,128)S(1)}, u32[]{:S(2)}, u32[]{:S(2)}) collective-permute-start(f32[4,1,2,36]{3,0,2,1:T(4,128)S(1)} %get-tuple-element.111), channel_id=1, source_target_pairs={{0,2},{2,4},{4,6},{1,3},{3,5},{5,7},{8,10},{10,12},{12,14},{9,11},... | collective-permute-start | bytes 3464 | tf_op jit(solution)/shard_map/ppermute | solution.py:25
  53.9 7.4 copy-start.26
  139.4 5.6 copy-start.15
  158.0 4.6 copy-start.2
  158.0 4.6 copy-start.13
  186.7 8.2 copy-start.3
  200.3 483.2 %all-reduce.12.cloned.1.call-start = ((), (), s32[]{:S(2)}) async-start(), calls=%async_computation | async-start | bytes 1572864
  215.4 273.2 %collective-permute-start.2 = (f32[4,4,1,36]{3,0,2,1:T(4,128)S(1)}, f32[4,4,1,36]{3,0,2,1:T(4,128)S(1)}, u32[]{:S(2)}, u32[]{:S(2)}) collective-permute-start(f32[4,4,1,36]{3,0,2,1:T(4,128)S(1)} %get-tuple-element.106), channel_id=1, source_target_pairs={{1,0},{3,2},{5,4},{7,6},{9,8},{11,10},{13,12},{15,14},{17,16},{19,... | collective-permute-start | bytes 6920 | tf_op jit(solution)/shard_map/ppermute | solution.py:27
  216.7 271.9 %collective-permute-start.3 = (f32[4,4,1,36]{3,0,2,1:T(4,128)S(1)}, f32[4,4,1,36]{3,0,2,1:T(4,128)S(1)}, u32[]{:S(2)}, u32[]{:S(2)}) collective-permute-start(f32[4,4,1,36]{3,0,2,1:T(4,128)S(1)} %get-tuple-element.107), channel_id=1, source_target_pairs={{0,1},{2,3},{4,5},{6,7},{8,9},{10,11},{12,13},{14,15},{16,17},{18,... | collective-permute-start | bytes 6920 | tf_op jit(solution)/shard_map/ppermute | solution.py:25
  366.4 4.9 copy-start.9
  366.4 4.9 copy-start.11
  405.9 11.7 %copy-start.6 = (f32[36,128,128]{2,1,0:T(8,128)S(1)}, f32[36,128,128]{2,1,0:T(8,128)}, u32[]{:S(2)}) copy-start(f32[36,128,128]{2,1,0:T(8,128)} %constant_dynamic-update-slice_fusion) | copy-start | bytes 7077892
  540.5 5.1 copy-start.19
  556.7 5.1 copy-start.1
  567.3 3.2 collective-permute-start.5
  569.1 4.4 collective-permute-start.4
  573.5 276.3 %collective-permute-start.6 = (f32[4,4,1,36]{3,0,2,1:T(4,128)S(1)}, f32[4,4,1,36]{3,0,2,1:T(4,128)S(1)}, u32[]{:S(2)}, u32[]{:S(2)}) collective-permute-start(f32[4,4,1,36]{3,0,2,1:T(4,128)S(1)} %get-tuple-element.100), channel_id=1, source_target_pairs={{1,0},{3,2},{5,4},{7,6},{9,8},{11,10},{13,12},{15,14},{17,16},{19,... | collective-permute-start | bytes 6920 | tf_op jit(solution)/shard_map/ppermute | solution.py:27
  574.8 275.0 %collective-permute-start.7 = (f32[4,4,1,36]{3,0,2,1:T(4,128)S(1)}, f32[4,4,1,36]{3,0,2,1:T(4,128)S(1)}, u32[]{:S(2)}, u32[]{:S(2)}) collective-permute-start(f32[4,4,1,36]{3,0,2,1:T(4,128)S(1)} %get-tuple-element.101), channel_id=1, source_target_pairs={{0,1},{2,3},{4,5},{6,7},{8,9},{10,11},{12,13},{14,15},{16,17},{18,... | collective-permute-start | bytes 6920 | tf_op jit(solution)/shard_map/ppermute | solution.py:25
  727.6 4.9 copy-start.8
  727.6 4.9 copy-start.10
  767.2 11.4 %copy-start.7 = (f32[36,128,128]{2,1,0:T(8,128)S(1)}, f32[36,128,128]{2,1,0:T(8,128)}, u32[]{:S(2)}) copy-start(f32[36,128,128]{2,1,0:T(8,128)} %constant_dynamic-update-slice_fusion) | copy-start | bytes 7077892
  (15 other events, 45.1 us)
Sparse Core Ops, SparseCore 0:
  200.4 121.6 all-reduce.13
  567.4 115.9 all-reduce.11
where the time goes:
time: 867 us; the launch traced here: 858 us
  matrix products  280 us (32%)
  blocking collectives  209 us (24%)
  waiting for transfers between devices  206 us (24%)
  other arithmetic  81.5 us (9%)
  local copies, waits for them, and re-layouts  39.4 us (5%)
  starting transfers between devices  23 us (3%)
  between operations  19.6 us (2%)
    unnamed x4, waiting for transfers between devices  203 us
    psum x2, blocking collectives, body(): total = lax.psum(jnp.sum(grads * grads), ('frame', 'row', 'col'))  129 us
    all_gather x2, blocking collectives, body(): lax.all_gather(object_imag, 'frame', axis=2, tiled=True)  41.3 us
    dot_general x4, matrix products, transform(): jnp.matmul(imag_part, cosine, precision=EXACT)  40.6 us
    all_gather x2, blocking collectives, body(): lax.all_gather(object_real, 'frame', axis=2, tiled=True)  38.4 us
    dot_general x9, matrix products, transform(): jnp.einsum('uy,...yx->...ux', cosine, half_imag, precision=EXACT)  36 us
    unnamed x34, other arithmetic  34.3 us
    dot_general x9, matrix products, transform(): jnp.einsum('uy,...yx->...ux', sine, half_imag, precision=EXACT)  28.1 us
  transfers between devices with their start and end apart: 10, of which 3 were waited for; matrix products, arithmetic and copies ran while one was open for 37% of the time, Pallas kernels for 0%

commit v1 on v0

v1 whole, which is shorter than its diff:
```python
import functools
import math

import jax
import jax.numpy as jnp
import ml_dtypes
import numpy as np
from jax import lax
from jax.experimental import pallas as pl
from jax.experimental.pallas import tpu as pltpu
from jax.sharding import PartitionSpec as P

ITERS = 2
MODES = 36
DIVERSITY = 1.5
TINY = 1e-06
PIXELS = 128
RADIUS = 32
SIDE = 72
PAD = 80
HALF = 64
FRAMES = 4
FIELDS = 4
ITEMS = FRAMES * FIELDS
UNITS = 16
F32 = jnp.float32
BF16 = jnp.bfloat16
MESH = pl.DeviceIdType.MESH


def noll_order(mode_index):
    radial_order = (math.isqrt(8 * (mode_index - 1) + 1) - 1) // 2
    position = mode_index - radial_order * (radial_order + 1) // 2
    parity = radial_order % 2
    azimuth = (position + parity) // 2 * 2 - parity
    if azimuth != 0 and mode_index % 2 == 1:
        azimuth = -azimuth
    return (radial_order, azimuth)


def zernike():
    line = np.arange(-RADIUS, RADIUS + 1) / RADIUS
    rows, cols = np.meshgrid(line, line, indexing="ij")
    radius = np.sqrt(rows * rows + cols * cols)
    angle = np.arctan2(rows, cols)
    mask = (rows * rows + cols * cols <= 1.0).astype(np.float64)
    shapes = []
    for mode_index in range(2, MODES + 2):
        n, m = noll_order(mode_index)
        radial = np.zeros_like(radius)
        for t in range((n - abs(m)) // 2 + 1):
            factor = (-1) ** t * math.factorial(n - t)
            factor /= math.factorial(t)
            factor /= math.factorial((n + abs(m)) // 2 - t)
            factor /= math.factorial((n - abs(m)) // 2 - t)
            radial = radial + factor * radius ** (n - 2 * t)
        if m == 0:
            shape = math.sqrt(n + 1) * radial
        elif m > 0:
            shape = math.sqrt(2 * (n + 1)) * radial * np.cos(m * angle)
        else:
            shape = math.sqrt(2 * (n + 1)) * radial * np.sin(-m * angle)
        shapes.append(shape * mask)
    return np.stack(shapes), mask


def pieces(values, count):
    out = []
    rest = np.asarray(values, np.float64)
    for _ in range(count):
        piece = rest.astype(np.float32).astype(ml_dtypes.bfloat16)
        out.append(piece)
        rest = rest - piece.astype(np.float64)
    return out


def right_table(matrix):
    hi, lo = pieces(matrix, 2)
    return np.concatenate([hi, lo, hi], axis=0)


def left_table(matrix):
    hi, lo = pieces(matrix, 2)
    return np.concatenate([hi, lo, hi], axis=1)


def tables():
    basis, mask = zernike()
    lit = mask.sum()
    turn = 2.0 * math.pi / PIXELS
    freq = np.arange(PIXELS)
    half = np.arange(HALF)
    pupil = np.arange(-RADIUS, RADIUS + 1)

    ang = turn * (pupil[:, None] * freq[None, :] % PIXELS)
    w1 = np.zeros((256, 256))
    w1[:65, :128] = np.cos(ang)
    w1[:65, 128:] = -np.sin(ang)
    w1[128 : 128 + 65, :128] = np.sin(ang)
    w1[128 : 128 + 65, 128:] = np.cos(ang)

    l2 = np.zeros((128, PAD))
    ang = turn * (half[:, None] * pupil[None, :] % PIXELS)
    l2[:64, :65] = np.cos(ang)
    l2[64:, :65] = np.sin(ang)
    l2[64, :65] = np.cos(turn * (64 * pupil % PIXELS))

    ang = turn * (half[:, None] * half[None, :] % PIXELS)
    q = np.zeros((128, 128))
    q[:64, :64] = 2.0 * np.cos(ang)
    q[64:, 64:] = -2.0 * np.sin(ang)
    q[:64, 0] = 1.0
    q[:64, 64] = (-1.0) ** half
    q[64, :] = 0.0
    q[64, 1:64] = 2.0 * (-1.0) ** half[1:]
    q[64, 0] = 1.0
    q[64, 64] = 1.0
    q = q / (lit * PIXELS * PIXELS)

    weight = np.full((128,), -8.0)
    weight[0] = -4.0
    weight[64] = -4.0
    qt = q.T * weight[None, :]

    qd = np.zeros((128, 128))
    ang = turn * (half[:, None] * freq[None, :] % PIXELS)
    qd[:64] = np.cos(ang)
    qd[64:] = -np.sin(ang)
    qd[64] = (-1.0) ** freq

    ang = turn * (freq[:, None] * freq[None, :] % PIXELS)
    w4 = np.zeros((256, 256))
    w4[:128, :128] = np.cos(ang)
    w4[:128, 128:] = -np.sin(ang)
    w4[128:, :128] = np.sin(ang)
    w4[128:, 128:] = np.cos(ang)

    wide = np.zeros((MODES, SIDE, 128))
    wide[:, :65, :65] = basis
    zh, zm, zl = pieces(wide, 3)
    phase = np.zeros((256, SIDE, 128), ml_dtypes.bfloat16)
    for at, part in ((0, zh), (36, zh), (72, zm), (128, zh), (164, zl), (200, zm)):
        phase[at : at + MODES] = part
    phase = phase.reshape(256, SIDE // 2, 256).transpose(1, 0, 2)

    grad = np.zeros((SIDE, 128, 128), ml_dtypes.bfloat16)
    grad[:, :, :MODES] = zh.transpose(1, 2, 0)
    grad[:, :, 64 : 64 + MODES] = zm.transpose(1, 2, 0)
    grad = grad.reshape(SIDE // 2, 256, 128)

    lens = np.zeros((3, SIDE, 128), np.float32)
    lens[0, :65, :65] = mask
    lens[1] = np.cos(DIVERSITY * wide[2])
    lens[2] = np.sin(DIVERSITY * wide[2])

    edges = np.minimum(freq, PIXELS - 1 - freq)
    taper = np.zeros((8, 128), np.float32)
    for kind in range(4):
        width = (kind + 1) * PIXELS // 16
        taper[kind] = np.where(
            edges < width, 0.5 - 0.5 * np.cos(math.pi * (edges + 0.5) / width), 1.0
        )

    flip = np.zeros((128, 128))
    flip[(-freq) % PIXELS, freq] = 1.0
    flip = np.concatenate([flip] * 3, axis=0).astype(ml_dtypes.bfloat16)

    return dict(
        w1=right_table(w1),
        w1t=right_table(w1.T),
        l2=left_table(l2),
        l2t=left_table(l2.T),
        q=left_table(q),
        qt=left_table(qt),
        w4=right_table(w4),
        w4t=right_table(w4.T),
        qd=qd.astype(np.float32),
        phase=phase,
        grad=grad,
        lens=lens,
        taper=taper,
        flip=flip,
    )


NAMES = (
    "w1", "w1t", "l2", "l2t", "q", "qt", "w4", "w4t", "qd", "phase", "grad", "lens", "taper", "flip",
)


def sincos(x):
    k = jnp.floor(x * np.float32(1.0 / math.pi) + 0.5)
    r = x - k * np.float32(3.140625)
    r = r - k * np.float32(0.0009670257568359375)
    r = r - k * np.float32(6.2771141529083251953e-7)
    odd = k - 2.0 * jnp.floor(k * 0.5)
    sign = 1.0 - 2.0 * odd
    r2 = r * r
    s = np.float32(-2.3868346521031027639830001794722295e-8)
    for c in (
        2.7526e-6,
        -1.98408735e-4,
        8.33333114e-3,
        -1.66666667e-1,
    ):
        s = s * r2 + np.float32(c)
    s = (s * r2 * r + r) * sign
    c_ = np.float32(-2.6e-7)
    for c in (
        2.4771e-5,
        -1.38888e-3,
        4.16666e-2,
        -0.5,
        1.0,
    ):
        c_ = c_ * r2 + np.float32(c)
    return s, c_ * sign


def two(x):
    hi = x.astype(BF16)
    return hi, (x - hi.astype(F32)).astype(BF16)


def right(x, table):
    hi, lo = two(x)
    return jnp.dot(jnp.concatenate([hi, hi, lo], axis=1), table, preferred_element_type=F32)


def left(table, x):
    hi, lo = two(x)
    return jnp.dot(table, jnp.concatenate([hi, hi, lo], axis=0), preferred_element_type=F32)


def patched(whole, first):
    return jnp.concatenate([first, whole[8:]], axis=0)


def kernel(
    nf, nr, nc,
    images, corners, kinds, coefs_in, step, noise, smooth,
    w1, w1t, l2, l2t, q, qt, w4, w4t, qd, phase_tab, grad_tab, lens, taper, flip,
    coefs_out, object_out,
    coefs, halo, phase, dphase, fields, waves, otf, data, rotor, sums, parts, objs, norm1, norm2, turned,
    rs_send, rs_recv, ag_send, ag_recv, n1_send, n1_recv, n2_send, n2_recv, h_send, h_recv,
):
    me = lax.axis_index("frame")
    row = lax.axis_index("row")
    col = lax.axis_index("col")
    place = row * nc + col
    nplace = nr * nc
    per = UNITS // nf

    lanes = lax.broadcasted_iota(jnp.int32, (8, 128), 1)
    subs = lax.broadcasted_iota(jnp.int32, (8, 128), 0)
    m00 = (lanes == 0) & (subs == 0)
    m064 = (lanes == 64) & (subs == 0)

    halo[...] = jnp.zeros(halo.shape, F32)

    npeers = (nf - 1) + (nplace - 1)
    if npeers:
        barrier = pltpu.get_barrier_semaphore()

        def greet_frame(k, _):
            peer = lax.rem(me + k, nf)
            pl.semaphore_signal(barrier, inc=1, device_id={"frame": peer}, device_id_type=MESH)
            return 0

        def greet_place(k, _):
            peer = lax.rem(place + k, nplace)
            pl.semaphore_signal(
                barrier, inc=1,
                device_id={"row": peer // nc, "col": lax.rem(peer, nc)}, device_id_type=MESH,
            )
            return 0

        lax.fori_loop(1, nf, greet_frame, 0)
        lax.fori_loop(1, nplace, greet_place, 0)

    coefs[...] = jnp.zeros((16, 128), F32)
    for f in range(FRAMES):
        for s in range(FIELDS):
            coefs[pl.ds(s * 4 + f, 1), pl.ds(0, MODES)] = coefs_in[f, s // 2, pl.ds(s % 2, 1), :]

    rows64 = lax.broadcasted_iota(jnp.int32, (HALF, 128), 0).astype(F32)
    cols8 = lanes.astype(F32)

    def data_field(s, _):
        kind = kinds[s // 2, lax.rem(s, 2)]
        window = jnp.where(
            kind == 0, taper[pl.ds(0, 1), :],
            jnp.where(
                kind == 1, taper[pl.ds(1, 1), :],
                jnp.where(kind == 2, taper[pl.ds(2, 1), :], taper[pl.ds(3, 1), :]),
            ),
        )
        hi, lo = two(qd[...] * window)
        rotor[:, pl.ds(0, 128)] = hi
        rotor[:, pl.ds(128, 128)] = lo

        def data_item(f, _):
            c0 = corners[0, f, s // 2, lax.rem(s, 2)].astype(F32)
            c1 = corners[1, f, s // 2, lax.rem(s, 2)].astype(F32)
            pair = jnp.concatenate(
                [images[f, s // 2, lax.rem(s, 2), 0], images[f, s // 2, lax.rem(s, 2), 1]], axis=1
            )
            lines = jnp.dot(
                rotor[...], jnp.concatenate([pair, pair], axis=0), preferred_element_type=F32
            )
            lines = lines * jnp.concatenate([window, window], axis=1)
            cycles = rows64 * (c0 * np.float32(1.0 / PIXELS))
            cycles = cycles - jnp.floor(cycles + 0.5)
            rs, rc = sincos(cycles * np.float32(2.0 * math.pi))
            cycles = cols8 * (c1 * np.float32(1.0 / PIXELS))
            cycles = cycles - jnp.floor(cycles + 0.5)
            cs, cc = sincos(cycles * np.float32(2.0 * math.pi))
            cs = cs[:1] * np.float32(1.0 / PIXELS)
            cc = cc[:1] * np.float32(1.0 / PIXELS)
            c0h = c0 * 0.5
            alternate = (1.0 - 4.0 * jnp.abs(c0h - jnp.floor(c0h))) * np.float32(1.0 / PIXELS)
            ready = []
            middle = []
            for c in range(2):
                zr = lines[:64, c * 128 : c * 128 + 128]
                zi = lines[64:, c * 128 : c * 128 + 128]
                middle.append(jnp.sum(zi[:1], axis=1, keepdims=True) * alternate)
                zi = patched(zi, jnp.where(subs == 0, 0.0, zi[:8]))
                ready.append(jnp.concatenate([zr * rc - zi * rs, zr * rs + zi * rc], axis=1))
            spec = right(jnp.concatenate(ready, axis=0), w4[...])
            for c in range(2):
                dr = spec[c * 64 : c * 64 + 64, :128]
                di = spec[c * 64 : c * 64 + 64, 128:]
                data[s * 4 + f, pl.ds(c * 64, 64), pl.ds(0, 128)] = dr * cc - di * cs
                di = dr * cs + di * cc
                data[s * 4 + f, pl.ds(c * 64, 64), pl.ds(128, 128)] = patched(
                    di, jnp.where(m00, middle[c], di[:8])
                )
            return 0

        lax.fori_loop(0, FRAMES, data_item, 0)
        return 0

    lax.fori_loop(0, FIELDS, data_field, 0)

    if npeers:
        pl.semaphore_wait(barrier, npeers)

    def rs_copy(it, h, peer):
        return pltpu.make_async_remote_copy(
            src_ref=sums.at[it, h, pl.ds(peer * per, per)],
            dst_ref=parts.at[it, h, me],
            send_sem=rs_send.at[it, h, peer],
            recv_sem=rs_recv.at[it, h, me],
            device_id={"frame": peer}, device_id_type=MESH,
        )

    def rs_arrival(it, h, peer):
        return pltpu.make_async_remote_copy(
            src_ref=sums.at[it, h, pl.ds(me * per, per)],
            dst_ref=parts.at[it, h, peer],
            send_sem=rs_send.at[it, h, peer],
            recv_sem=rs_recv.at[it, h, peer],
            device_id={"frame": peer}, device_id_type=MESH,
        )

    def ag_copy(it, h, peer):
        return pltpu.make_async_remote_copy(
            src_ref=objs.at[it, h, pl.ds(me * per, per)],
            dst_ref=objs.at[it, h, pl.ds(me * per, per)],
            send_sem=ag_send.at[it, h, peer],
            recv_sem=ag_recv.at[it, h, me],
            device_id={"frame": peer}, device_id_type=MESH,
        )

    def ag_arrival(it, h, peer):
        return pltpu.make_async_remote_copy(
            src_ref=objs.at[it, h, pl.ds(peer * per, per)],
            dst_ref=objs.at[it, h, pl.ds(peer * per, per)],
            send_sem=ag_send.at[it, h, peer],
            recv_sem=ag_recv.at[it, h, peer],
            device_id={"frame": peer}, device_id_type=MESH,
        )

    def n1_copy(it, peer, slot):
        return pltpu.make_async_remote_copy(
            src_ref=norm1.at[it, me],
            dst_ref=norm1.at[it, slot],
            send_sem=n1_send.at[it, peer],
            recv_sem=n1_recv.at[it, slot],
            device_id={"frame": peer}, device_id_type=MESH,
        )

    def n2_copy(it, peer, slot):
        return pltpu.make_async_remote_copy(
            src_ref=norm2.at[it, place],
            dst_ref=norm2.at[it, slot],
            send_sem=n2_send.at[it, peer],
            recv_sem=n2_recv.at[it, slot],
            device_id={"row": peer // nc, "col": lax.rem(peer, nc)}, device_id_type=MESH,
        )

    def halo_copies(it):
        def one(axis, index, count, delta, src, slot):
            peer = jnp.clip(index + delta, 0, count - 1)
            there = (index + delta >= 0) & (index + delta < count)
            return there, pltpu.make_async_remote_copy(
                src_ref=src,
                dst_ref=halo.at[it, slot],
                send_sem=h_send.at[it, slot],
                recv_sem=h_recv.at[it, slot],
                device_id={axis: peer}, device_id_type=MESH,
            )

        src = halo.at[it, 4]
        out = []
        if nr > 1:
            out.append(one("row", row, nr, 1, src, 0))
            out.append(one("row", row, nr, -1, src, 1))
        if nc > 1:
            out.append(one("col", col, nc, 1, src, 2))
            out.append(one("col", col, nc, -1, src, 3))
        return out

    def halo_sides(it):
        out = []
        if nr > 1:
            out += [(0, row > 0), (1, row < nr - 1)]
        if nc > 1:
            out += [(2, col > 0), (3, col < nc - 1)]
        return out

    def each_peer(count, mine, act):
        if count > 1:
            def body(k, _):
                act(lax.rem(mine + k, count))
                return 0

            lax.fori_loop(1, count, body, 0)

    def reduce_pair(it, h):
        each_peer(nf, me, lambda peer: rs_arrival(it, h, peer).wait_recv())
        for j in range(per):
            unit = me * per + j
            total = sums[it, h, unit]

            def add(k, total):
                return total + parts[it, h, lax.rem(me + k, nf), j]

            if nf > 1:
                total = lax.fori_loop(1, nf, add, total)
            first = lax.rem(unit, 8) == 0
            real, imag, power = total[0], total[1], total[2]
            n = noise[0, 0]
            other = jnp.where(m00 & first, pltpu.roll(imag, 64, 1), power)
            objs[it, h, unit, 0] = real / (power + n)
            objs[it, h, unit, 1] = jnp.where(m064 & first, 0.0, imag / (other + n))
        each_peer(nf, me, lambda peer: ag_copy(it, h, peer).start())

    def forward(it, s, f):
        item = s * 4 + f
        sin0, cos0 = sincos(phase[pl.ds(item, SIDE, stride=16), :])
        mask = lens[0]
        cos0 = cos0 * mask
        sin0 = sin0 * mask
        cos1 = cos0 * lens[1] - sin0 * lens[2]
        sin1 = sin0 * lens[1] + cos0 * lens[2]
        fields[item, 0] = cos0
        fields[item, 1] = sin0
        fields[item, 2] = cos1
        fields[item, 3] = sin1
        none = jnp.zeros((PAD - SIDE, 256), F32)
        pupil = jnp.concatenate(
            [
                jnp.concatenate([cos0, sin0], axis=1), none,
                jnp.concatenate([cos1, sin1], axis=1), none,
            ],
            axis=0,
        )
        lines = right(pupil, w1[...])
        evens = []
        odds = []
        for c in range(2):
            wave = left(l2[...], lines[c * PAD : c * PAD + PAD])
            waves[item, c] = wave
            a, b = wave[:64, :128], wave[:64, 128:]
            e, d = wave[64:, :128], wave[64:, 128:]
            ab = a * a + b * b
            ed = e * e + d * d
            even = ab + ed
            odd = 2.0 * (a * d - b * e)
            evens.append(patched(even, jnp.where(subs == 0, ab[:8], even[:8])))
            odds.append(patched(odd, jnp.where(subs == 0, ed[:8], odd[:8])))
        spread = jnp.concatenate(
            [jnp.concatenate(evens, axis=1), jnp.concatenate(odds, axis=1)], axis=0
        )
        lines = left(q[...], spread)
        z = jnp.concatenate(
            [
                jnp.concatenate([lines[:64, c * 128 : c * 128 + 128], lines[64:, c * 128 : c * 128 + 128]], axis=1)
                for c in range(2)
            ],
            axis=0,
        )
        z = right(z, w4[...])
        otf[item] = z
        d = data[item]
        h = s // 2
        base = lax.rem(s, 2) * 8
        for t in range(8):
            cr = ci = pw = None
            for c in range(2):
                at = slice(c * 64 + t * 8, c * 64 + t * 8 + 8)
                zr, zi, dr, di = z[at, :128], z[at, 128:], d[at, :128], d[at, 128:]
                ii = zi * di
                zz = zi * zi
                im = zr * di - zi * dr
                if t == 0:
                    im = jnp.where(m00, ii, im)
                    im = jnp.where(m064, pltpu.roll(zz, 64, 1), im)
                    ii = jnp.where(m00, 0.0, ii)
                    zz = jnp.where(m00, 0.0, zz)
                re = zr * dr + ii
                p = zr * zr + zz
                cr = re if cr is None else cr + re
                ci = im if ci is None else ci + im
                pw = p if pw is None else pw + p
            sums[it, h, base + t, 0] += cr
            sums[it, h, base + t, 1] += ci
            sums[it, h, base + t, 2] += pw

    def backward(it, s, f):
        item = s * 4 + f
        h = s // 2
        base = lax.rem(s, 2) * 8
        z = otf[item]
        d = data[item]
        res = [[], []]
        for t in range(8):
            our = objs[it, h, base + t, 0]
            oui = objs[it, h, base + t, 1]
            for c in range(2):
                at = slice(c * 64 + t * 8, c * 64 + t * 8 + 8)
                zr, zi, dr, di = z[at, :128], z[at, 128:], d[at, :128], d[at, 128:]
                ii = oui * zi
                ri = oui * zr
                rr = our * zi
                if t == 0:
                    rr = jnp.where(m00, ii, rr)
                    ri = jnp.where(m00, 0.0, ri)
                    ii = jnp.where(m00, 0.0, ii)
                er = dr - (our * zr - ii)
                ei = di - (rr + ri)
                x = ei * oui
                y = ei * our
                w = er * oui
                if t == 0:
                    y = jnp.where(m00, x, y)
                    x = jnp.where(m00, 0.0, x)
                    w = jnp.where(m00, 0.0, w)
                res[c].append(jnp.concatenate([er * our + x, y - w], axis=1))
        dz = right(jnp.concatenate(res[0] + res[1], axis=0), w4t[...])
        lines = jnp.concatenate(
            [
                jnp.concatenate([dz[:64, :128], dz[64:, :128]], axis=1),
                jnp.concatenate([dz[:64, 128:], dz[64:, 128:]], axis=1),
            ],
            axis=0,
        )
        dspread = left(qt[...], lines)
        dlines = []
        for c in range(2):
            de = dspread[:64, c * 128 : c * 128 + 128]
            do = dspread[64:, c * 128 : c * 128 + 128]
            wave = waves[item, c]
            a, b = wave[:64, :128], wave[:64, 128:]
            e, d_ = wave[64:, :128], wave[64:, 128:]
            da = a * de + d_ * do
            db = b * de - e * do
            dc = e * de - b * do
            dd = d_ * de + a * do
            de8, do8 = de[:8], do[:8]
            zero = subs == 0
            da = patched(da, jnp.where(zero, a[:8] * de8, da[:8]))
            db = patched(db, jnp.where(zero, b[:8] * de8, db[:8]))
            dc = patched(dc, jnp.where(zero, e[:8] * do8, dc[:8]))
            dd = patched(dd, jnp.where(zero, d_[:8] * do8, dd[:8]))
            dwave = jnp.concatenate(
                [jnp.concatenate([da, db], axis=1), jnp.concatenate([dc, dd], axis=1)], axis=0
            )
            dlines.append(left(l2t[...], dwave))
        dpupil = right(jnp.concatenate(dlines, axis=0), w1t[...])
        total = None
        for c in range(2):
            part = (
                fields[item, 2 * c] * dpupil[c * PAD : c * PAD + SIDE, 128:]
                - fields[item, 2 * c + 1] * dpupil[c * PAD : c * PAD + SIDE, :128]
            )
            total = part if total is None else total + part
        dphase[pl.ds(item, SIDE, stride=16), :] = total

    def all_frames(act, it, s):
        def body(f, _):
            act(it, s, f)
            return 0

        lax.fori_loop(0, FRAMES, body, 0)

    def send_pair(it, h):
        each_peer(nf, me, lambda peer: rs_copy(it, h, peer).start())

    def iteration(it, _):
        halo[it, 4] = coefs[...]
        for there, copy in halo_copies(it):
            pl.when(there)(copy.start)

        cf = coefs[...]
        ch = cf.astype(BF16).astype(F32)
        cm = (cf - ch).astype(BF16).astype(F32)
        cl = (cf - ch - cm).astype(BF16).astype(F32)
        low = ch + pltpu.roll(cm, 36, 1) + pltpu.roll(ch, 72, 1)
        high = cl + pltpu.roll(ch, 36, 1) + pltpu.roll(cm, 72, 1)
        lhs = jnp.concatenate([low, high], axis=1).astype(BF16)

        def phase_rows(j, _):
            out = jnp.dot(lhs, phase_tab[j], preferred_element_type=F32)
            at = pl.multiple_of(j * 32, 32)
            phase[pl.ds(at, 16), :] = out[:, :128]
            phase[pl.ds(at + 16, 16), :] = out[:, 128:]
            return 0

        lax.fori_loop(0, SIDE // 2, phase_rows, 0)
        sums[it] = jnp.zeros(sums.shape[1:], F32)

        all_frames(forward, it, 0)
        all_frames(forward, it, 1)
        send_pair(it, 0)
        all_frames(forward, it, 2)
        reduce_pair(it, 0)
        all_frames(forward, it, 3)
        send_pair(it, 1)
        each_peer(nf, me, lambda peer: ag_arrival(it, 0, peer).wait_recv())
        all_frames(backward, it, 0)
        reduce_pair(it, 1)
        all_frames(backward, it, 1)
        each_peer(nf, me, lambda peer: ag_arrival(it, 1, peer).wait_recv())
        all_frames(backward, it, 2)
        all_frames(backward, it, 3)

        def grad_rows(j, acc):
            at = pl.multiple_of(j * 32, 32)
            x = jnp.concatenate([dphase[pl.ds(at, 16), :], dphase[pl.ds(at + 16, 16), :]], axis=1)
            hi, lo = two(x)
            return acc + jnp.dot(
                jnp.concatenate([hi, lo], axis=0), grad_tab[j], preferred_element_type=F32
            )

        acc = lax.fori_loop(0, SIDE // 2, grad_rows, jnp.zeros((32, 128), F32))
        grads = acc[:16] + pltpu.roll(acc[:16], 64, 1) + acc[16:]
        lane16 = lax.broadcasted_iota(jnp.int32, (16, 128), 1)
        grads = jnp.where(lane16 < MODES, grads, 0.0)

        sq = grads * grads
        norm1[it, me] = jnp.sum(sq[:8] + sq[8:], axis=0, keepdims=True)
        each_peer(nf, me, lambda peer: n1_copy(it, peer, me).start())
        each_peer(nf, me, lambda peer: n1_copy(it, peer, peer).wait_recv())
        norm2[it, place] = jnp.sum(norm1[it], axis=0)
        each_peer(nplace, place, lambda peer: n2_copy(it, peer, place).start())

        for slot, there in halo_sides(it):
            @pl.when(there)
            def _(slot=slot):
                pltpu.make_async_copy(halo.at[it, slot], halo.at[it, slot], h_recv.at[it, slot]).wait()

        above, below = halo[it, 0, 8:], halo[it, 1, :8]
        laplace = []
        for r in range(2):
            own = cf[r * 8 : r * 8 + 8]
            other = cf[8 - r * 8 : 16 - r * 8]
            beside = jnp.where(
                subs < 4,
                pltpu.roll(halo[it, 2, r * 8 : r * 8 + 8], 4, 0),
                pltpu.roll(halo[it, 3, r * 8 : r * 8 + 8], 4, 0),
            )
            out = 4.0 * own - other - pltpu.roll(own, 4, 0) - beside
            laplace.append(out - (above if r == 0 else below))
        laplace = jnp.concatenate(laplace, axis=0)

        each_peer(nplace, place, lambda peer: n2_copy(it, peer, peer).wait_recv())
        total = jnp.sum(jnp.sum(norm2[it], axis=0), axis=1, keepdims=True)
        count = ITEMS * MODES * nf * nplace
        scale = jnp.sqrt(total / count + TINY)
        coefs[...] = cf - step[0, 0] * (grads / scale + smooth[0, 0] * laplace)

        for h in range(2):
            each_peer(nf, me, lambda peer: rs_copy(it, h, peer).wait_send())
            each_peer(nf, me, lambda peer: ag_copy(it, h, peer).wait_send())
        each_peer(nf, me, lambda peer: n1_copy(it, peer, me).wait_send())
        each_peer(nplace, place, lambda peer: n2_copy(it, peer, place).wait_send())
        for there, copy in halo_copies(it):
            pl.when(there)(copy.wait_send)
        return 0

    lax.fori_loop(0, ITERS, iteration, 0)

    for f in range(FRAMES):
        for s in range(FIELDS):
            coefs_out[f, s // 2, pl.ds(s % 2, 1), :] = coefs[pl.ds(s * 4 + f, 1), pl.ds(0, MODES)]

    last = ITERS - 1
    for j in range(per):
        tile = me * per + j

        @pl.when(tile < 8)
        def _(j=j, tile=tile):
            for s in range(FIELDS):
                re = objs[last, s // 2, s % 2 * 8 + tile, 0]
                im = objs[last, s // 2, s % 2 * 8 + tile, 1]
                object_out[0, s // 2, s % 2, pl.ds(j * 8, 8), :] = re
                object_out[1, s // 2, s % 2, pl.ds(j * 8, 8), :] = jnp.where(m00 & (tile == 0), 0.0, im)

        @pl.when(tile >= 8)
        def _(j=j, tile=tile):
            g = tile - 8
            for s in range(FIELDS):
                base = s % 2 * 8
                for c in range(2):
                    at = (s * 2 + c) * 8
                    for i in range(1, 8):
                        turned[pl.ds(at + i, 1), :] = objs[last, s // 2, base + 7 - g, c, pl.ds(8 - i, 1), :]
                    zero = objs[last, s // 2, base + lax.rem(8 - g, 8), c, pl.ds(0, 1), :]
                    if c == 0:
                        middle = objs[last, s // 2, base, 1, pl.ds(0, 1), :]
                        middle = jnp.where(lanes[:1] == 0, middle, 0.0)
                    else:
                        middle = jnp.zeros((1, 128), F32)
                    turned[pl.ds(at, 1), :] = jnp.where(g == 0, middle, zero)
            x = turned[...]
            h = x.astype(BF16)
            rest = x - h.astype(F32)
            m = rest.astype(BF16)
            l = (rest - m.astype(F32)).astype(BF16)
            out = jnp.dot(jnp.concatenate([h, m, l], axis=1), flip[...], preferred_element_type=F32)
            for s in range(FIELDS):
                at = s * 16
                object_out[0, s // 2, s % 2, pl.ds(j * 8, 8), :] = out[at : at + 8]
                object_out[1, s // 2, s % 2, pl.ds(j * 8, 8), :] = -out[at + 8 : at + 16]


def solution(mesh):
    nf, nr, nc = (mesh.shape[name] for name in ("frame", "row", "col"))
    host = tables()
    per = UNITS // nf
    vmem = pl.BlockSpec(memory_space=pltpu.VMEM)
    smem = pl.BlockSpec(memory_space=pltpu.SMEM)

    def body(images, corners, kinds, coefs, step, noise, smooth):
        scratch = [
            pltpu.VMEM((16, 128), F32),
            pltpu.VMEM((ITERS, 5, 16, 128), F32),
            pltpu.VMEM((SIDE * 16, 128), F32),
            pltpu.VMEM((SIDE * 16, 128), F32),
            pltpu.VMEM((ITEMS, 4, SIDE, 128), F32),
            pltpu.VMEM((ITEMS, 2, 128, 256), F32),
            pltpu.VMEM((ITEMS, 128, 256), F32),
            pltpu.VMEM((ITEMS, 128, 256), F32),
            pltpu.VMEM((128, 256), BF16),
            pltpu.VMEM((ITERS, 2, UNITS, 3, 8, 128), F32),
            pltpu.VMEM((ITERS, 2, nf, per, 3, 8, 128), F32),
            pltpu.VMEM((ITERS, 2, UNITS, 2, 8, 128), F32),
            pltpu.VMEM((ITERS, nf, 1, 128), F32),
            pltpu.VMEM((ITERS, nr * nc, 1, 128), F32),
            pltpu.VMEM((HALF, 128), F32),
        ]
        dma = pltpu.SemaphoreType.DMA
        scratch += [dma((ITERS, 2, nf)) for _ in range(4)]
        scratch += [dma((ITERS, nf)) for _ in range(2)]
        scratch += [dma((ITERS, nr * nc)) for _ in range(2)]
        scratch += [dma((ITERS, 4)) for _ in range(2)]
        single = lambda x: x.reshape(1, 1)
        return pl.pallas_call(
            functools.partial(kernel, nf, nr, nc),
            out_shape=(
                jax.ShapeDtypeStruct((FRAMES, 2, 2, MODES), F32),
                jax.ShapeDtypeStruct((2, 2, 2, 8 * per, 128), F32),
            ),
            in_specs=[vmem, smem, smem, vmem, smem, smem, smem] + [vmem] * len(NAMES),
            out_specs=(vmem, vmem),
            scratch_shapes=scratch,
            compiler_params=pltpu.CompilerParams(
                collective_id=0 if nf * nr * nc > 1 else None,
                has_side_effects=True,
                vmem_limit_bytes=56 * 1024 * 1024,
            ),
        )(
            images, corners, kinds, coefs, single(step), single(noise), single(smooth),
            *[jnp.asarray(host[name]) for name in NAMES],
        )

    in_specs = (
        P("frame", "row", "col", None, None, None),
        P(None, "frame", "row", "col"),
        P("row", "col"),
        P("frame", "row", "col", None),
        P(),
        P(),
        P(),
    )
    out_specs = (P("frame", "row", "col", None), P(None, "row", "col", "frame", None))
    return jax.shard_map(body, mesh=mesh, in_specs=in_specs, out_specs=out_specs, check_vma=False)
```

time: 867 us -> 130 us (0.15)
  matrix products: 280 us -> 0 us
  blocking collectives: 209 us -> 0 us
  waiting for transfers between devices: 206 us -> 0 us
  Pallas kernels: 0 us -> 123 us
  other arithmetic: 81.5 us -> 0 us
  local copies, waits for them, and re-layouts: 39.4 us -> 4.05 us
  starting transfers between devices: 23 us -> 0 us
  between operations: 19.6 us -> 2.58 us
    dot_general x67 -> x0, matrix products: 280 us -> none  [the longest x4 40.6 us: transform(): jnp.matmul(imag_part, cosine, precision=EXACT)]
    unnamed x4 -> x0, waiting for transfers between devices: 203 us -> none
    psum x2 -> x0, blocking collectives: 129 us -> none  [body(): total = lax.psum(jnp.sum(grads * grads), ('frame', 'row', 'col'))]
    pallas_call x0 -> x1, Pallas kernels: none -> 123 us  [body(): pl.pallas_call(functools.partial(kernel, nf, nr, nc), out_shape=(jax.Shap...]
    all_gather x4 -> x0, blocking collectives: 79.7 us -> none  [the longest x2 41.3 us: body(): lax.all_gather(object_imag, 'frame', axis=2, tiled=True)]
    unnamed x34 -> x0, other arithmetic: 34.3 us -> none
    mul x8 -> x0, other arithmetic: 23.3 us -> none  [the longest x5 22.1 us: zernike_table(): shapes.append(mode_shape * pupil_mask)]
    ppermute x8 -> x0, starting transfers between devices: 23 us -> none  [the longest x4 17.8 us: padded_2(): lax.ppermute(tail, axis, [(i, (i + 1) % count) for i in range(ends)])]
  transfers between devices with their start and end apart: 10 -> 0, of which waited for: 3 -> 0; matrix products, arithmetic and copies ran while one was open for 37% -> 0% of each run, Pallas kernels for 0% -> 0%
where the time goes in v1:
time: 130 us; the launch traced here: 129 us
  Pallas kernels  123 us (95%)
  local copies, waits for them, and re-layouts  4.05 us (3%)
  between operations  2.58 us (2%)
    pallas_call x1, Pallas kernels, body(): pl.pallas_call(functools.partial(kernel, nf, nr, nc), out_shape=(jax.Shap...  123 us
    unnamed x3, local copies, waits for them, and re-layouts  4.05 us

profile of v1, /device:TPU:1, one launch (start us, length us, event | category | flops | bytes accessed | tf_op | source)
XLA Modules:
  0.0 129.3 jit_solution(15161247377540902485)
XLA Ops:
  2.6 1.4 %copy.23.corners = s32[2,4,2,2]{3,2,1,0:T(2,128)} copy(s32[2,4,2,2]{1,3,2,0:T(2,128)} %param.22) | data formatting | bytes 256 | tf_op args[1]
  4.0 122.6 %shard_map.212 = (f32[4,2,2,36]{3,2,1,0:T(2,128)}, f32[2,2,2,8,128]{4,3,2,1,0:T(8,128)}) custom-call(bf16[4,2,2,2,128,128]{5,4,3,2,1,0:T(8,128)(2,1)} %images.1, s32[2,4,2,2]{3,2,1,0:T(2,128)} %copy.23.corners, s32[2,2]{1,0:T(2,128)} %kinds.1, f32[4,2,2,36]{3,2,1,0:T(2,128)} %coefs_in.1, f32[1,1]{1,0:T(1,128)} %bitcast.3.step, f32[1,1]{1,0:T(1,128)} %bitcast.4.noise, ...), custom_call_target="tpu_custom_call" | custom-call | tf_op jit(solution)/shard_map/pallas_call | solution.py:781
  126.6 1.3 %copy.29 = f32[4,2,2,36]{3,2,1,0:T(2,128)} copy(f32[4,2,2,36]{3,2,1,0:T(2,128)} %get-tuple-element.4) | data formatting | bytes 4608
  127.9 1.4 %copy.30 = f32[2,2,2,8,128]{4,3,2,1,0:T(8,128)} copy(f32[2,2,2,8,128]{4,3,2,1,0:T(8,128)} %get-tuple-element.5) | data formatting | bytes 65536

commit v2 on v1

v2 whole, which is shorter than its diff:
```python
import functools
import math

import jax
import jax.numpy as jnp
import ml_dtypes
import numpy as np
from jax import lax
from jax.experimental import pallas as pl
from jax.experimental.pallas import tpu as pltpu
from jax.sharding import PartitionSpec as P

ITERS = 2
MODES = 36
DEGREE = 9
DIVERSITY = 1.5
TINY = 1e-06
PIXELS = 128
RADIUS = 32
SIDE = 72
PAD = 80
HALF = 64
FRAMES = 4
FIELDS = 4
ITEMS = FRAMES * FIELDS
TILES = 8
F32 = jnp.float32
BF16 = jnp.bfloat16
MESH = pl.DeviceIdType.MESH


def noll_order(mode_index):
    radial_order = (math.isqrt(8 * (mode_index - 1) + 1) - 1) // 2
    position = mode_index - radial_order * (radial_order + 1) // 2
    parity = radial_order % 2
    azimuth = (position + parity) // 2 * 2 - parity
    if azimuth != 0 and mode_index % 2 == 1:
        azimuth = -azimuth
    return (radial_order, azimuth)


def zernike():
    line = np.arange(-RADIUS, RADIUS + 1) / RADIUS
    rows, cols = np.meshgrid(line, line, indexing="ij")
    radius = np.sqrt(rows * rows + cols * cols)
    angle = np.arctan2(rows, cols)
    mask = (rows * rows + cols * cols <= 1.0).astype(np.float64)
    shapes = []
    for mode_index in range(2, MODES + 2):
        n, m = noll_order(mode_index)
        radial = np.zeros_like(radius)
        for t in range((n - abs(m)) // 2 + 1):
            factor = (-1) ** t * math.factorial(n - t)
            factor /= math.factorial(t)
            factor /= math.factorial((n + abs(m)) // 2 - t)
            factor /= math.factorial((n - abs(m)) // 2 - t)
            radial = radial + factor * radius ** (n - 2 * t)
        if m == 0:
            shape = math.sqrt(n + 1) * radial
        elif m > 0:
            shape = math.sqrt(2 * (n + 1)) * radial * np.cos(m * angle)
        else:
            shape = math.sqrt(2 * (n + 1)) * radial * np.sin(-m * angle)
        shapes.append(shape)
    return np.stack(shapes), mask


def pieces(values, count):
    out = []
    rest = np.asarray(values, np.float64)
    for _ in range(count):
        piece = rest.astype(np.float32).astype(ml_dtypes.bfloat16)
        out.append(piece)
        rest = rest - piece.astype(np.float64)
    return out


def right_table(matrix):
    hi, lo = pieces(matrix, 2)
    return np.concatenate([hi, lo, hi], axis=0)


def left_table(matrix):
    hi, lo = pieces(matrix, 2)
    return np.concatenate([hi, lo, hi], axis=1)


def tables():
    modes, mask = zernike()
    lit = mask.sum()
    turn = 2.0 * math.pi / PIXELS
    freq = np.arange(PIXELS)
    half = np.arange(HALF)
    pupil = np.arange(-RADIUS, RADIUS + 1)

    ang = turn * (pupil[:, None] * freq[None, :] % PIXELS)
    w1 = np.zeros((256, 256))
    w1[:65, :128] = np.cos(ang)
    w1[:65, 128:] = -np.sin(ang)
    w1[128 : 128 + 65, :128] = np.sin(ang)
    w1[128 : 128 + 65, 128:] = np.cos(ang)

    l2 = np.zeros((128, PAD))
    ang = turn * (half[:, None] * pupil[None, :] % PIXELS)
    l2[:64, :65] = np.cos(ang)
    l2[64:, :65] = np.sin(ang)
    l2[64, :65] = np.cos(turn * (64 * pupil % PIXELS))

    ang = turn * (half[:, None] * half[None, :] % PIXELS)
    q = np.zeros((128, 128))
    q[:64, :64] = 2.0 * np.cos(ang)
    q[64:, 64:] = -2.0 * np.sin(ang)
    q[:64, 0] = 1.0
    q[:64, 64] = (-1.0) ** half
    q[64, :] = 0.0
    q[64, 1:64] = 2.0 * (-1.0) ** half[1:]
    q[64, 0] = 1.0
    q[64, 64] = 1.0
    q = q / (lit * PIXELS * PIXELS)

    weight = np.full((128,), -8.0)
    weight[0] = -4.0
    weight[64] = -4.0
    qt = q.T * weight[None, :]

    qd = np.zeros((128, 128))
    ang = turn * (half[:, None] * freq[None, :] % PIXELS)
    qd[:64] = np.cos(ang)
    qd[64:] = -np.sin(ang)
    qd[64] = (-1.0) ** freq

    ang = turn * (freq[:, None] * freq[None, :] % PIXELS)
    w4 = np.zeros((256, 256))
    w4[:128, :128] = np.cos(ang)
    w4[:128, 128:] = -np.sin(ang)
    w4[128:, :128] = np.sin(ang)
    w4[128:, 128:] = np.cos(ang)

    rows_table = np.polynomial.legendre.legvander(pupil / RADIUS, DEGREE - 1)
    t = np.zeros((MODES, DEGREE, 128))
    t[:, :, :65] = np.einsum("ip,kpx->kix", np.linalg.pinv(rows_table), modes)
    th, tm, tl = pieces(t, 3)
    t1 = np.zeros((256, DEGREE * 128), ml_dtypes.bfloat16)
    for at, part in ((0, th), (36, th), (72, tm), (128, th), (164, tl), (200, tm)):
        t1[at : at + MODES] = part.reshape(MODES, -1)
    t2 = np.zeros((DEGREE * 128, 128), ml_dtypes.bfloat16)
    t2[:, :MODES] = th.reshape(MODES, -1).T
    t2[:, 64 : 64 + MODES] = tm.reshape(MODES, -1).T

    y = np.zeros((SIDE, 16))
    y[:65, :DEGREE] = rows_table
    yh, ym, yl = pieces(y, 3)
    y1 = np.concatenate([yh, yh, ym, yh, yl, ym], axis=1)
    y = np.zeros((16, PAD))
    y[:DEGREE, :65] = rows_table.T
    y2 = left_table(y)

    lens = np.zeros((3, SIDE, 128), np.float32)
    lens[0, :65, :65] = mask
    lens[1, :65, :65] = np.cos(DIVERSITY * modes[2] * mask)
    lens[2, :65, :65] = np.sin(DIVERSITY * modes[2] * mask)

    edges = np.minimum(freq, PIXELS - 1 - freq)
    taper = np.zeros((8, 128), np.float32)
    for kind in range(4):
        width = (kind + 1) * PIXELS // 16
        taper[kind] = np.where(
            edges < width, 0.5 - 0.5 * np.cos(math.pi * (edges + 0.5) / width), 1.0
        )

    flip = np.zeros((128, 128))
    flip[(-freq) % PIXELS, freq] = 1.0
    flip = np.concatenate([flip] * 3, axis=0).astype(ml_dtypes.bfloat16)

    return dict(
        w1=right_table(w1),
        w1t=right_table(w1.T),
        l2=left_table(l2),
        l2t=left_table(l2.T),
        q=left_table(q),
        qt=left_table(qt),
        w4=right_table(w4),
        w4t=right_table(w4.T),
        qd=qd.astype(np.float32),
        t1=t1,
        t2=t2,
        y1=y1,
        y2=y2,
        lens=lens,
        taper=taper,
        flip=flip,
    )


NAMES = (
    "w1", "w1t", "l2", "l2t", "q", "qt", "w4", "w4t", "qd", "t1", "t2", "y1", "y2", "lens", "taper", "flip",
)


def sincos(x):
    k = jnp.floor(x * np.float32(1.0 / math.pi) + 0.5)
    r = x - k * np.float32(3.140625)
    r = r - k * np.float32(0.0009670257568359375)
    r = r - k * np.float32(6.2771141529083251953e-7)
    odd = k - 2.0 * jnp.floor(k * 0.5)
    sign = 1.0 - 2.0 * odd
    r2 = r * r
    s = np.float32(-2.3868346521031027639830001794722295e-8)
    for c in (
        2.7526e-6,
        -1.98408735e-4,
        8.33333114e-3,
        -1.66666667e-1,
    ):
        s = s * r2 + np.float32(c)
    s = (s * r2 * r + r) * sign
    c_ = np.float32(-2.6e-7)
    for c in (
        2.4771e-5,
        -1.38888e-3,
        4.16666e-2,
        -0.5,
        1.0,
    ):
        c_ = c_ * r2 + np.float32(c)
    return s, c_ * sign


def two(x):
    hi = x.astype(BF16)
    return hi, (x - hi.astype(F32)).astype(BF16)


def three(x):
    hi = x.astype(BF16)
    rest = x - hi.astype(F32)
    mid = rest.astype(BF16)
    return hi, mid, (rest - mid.astype(F32)).astype(BF16)


def right(x, table):
    hi, lo = two(x)
    return jnp.dot(jnp.concatenate([hi, hi, lo], axis=1), table, preferred_element_type=F32)


def left(table, x):
    hi, lo = two(x)
    return jnp.dot(table, jnp.concatenate([hi, hi, lo], axis=0), preferred_element_type=F32)


def patched(whole, first):
    return jnp.concatenate([first, whole[8:]], axis=0)


def kernel(
    nf, nr, nc,
    images, corners, kinds, coefs_in, step, noise, smooth,
    w1, w1t, l2, l2t, q, qt, w4, w4t, qd, t1, t2, y1, y2, lens, taper, flip,
    coefs_out, object_out,
    coefs, halo, bent, dbent, fields, waves, otf, data, sums, parts, objs, norm1, norm2, turned,
    rs_send, rs_recv, ag_send, ag_recv, n1_send, n1_recv, n2_send, n2_recv, h_send, h_recv,
):
    me = lax.axis_index("frame")
    row = lax.axis_index("row")
    col = lax.axis_index("col")
    place = row * nc + col
    nplace = nr * nc
    per = 16 // nf
    own = min(per, TILES)
    owners = TILES // own
    pair = nf // 2
    chips = max(pair, 1) * nplace

    lanes = lax.broadcasted_iota(jnp.int32, (8, 128), 1)
    subs = lax.broadcasted_iota(jnp.int32, (8, 128), 0)
    m00 = (lanes == 0) & (subs == 0)
    m064 = (lanes == 64) & (subs == 0)

    def loop(first, last, act):
        def body(k, _):
            act(k)
            return 0

        if last > first:
            lax.fori_loop(first, last, body, 0)

    halo[...] = jnp.zeros(halo.shape, F32)

    def chip_at(k):
        mine = me // 2 * nplace + place
        chip = lax.rem(mine + k, chips)
        return chip // nplace * 2 + lax.rem(me, 2), lax.rem(chip, nplace)

    def there(frame, where):
        return {"frame": frame, "row": where // nc, "col": lax.rem(where, nc)}

    npeers = (nf - 1) + max(pair, 1) * (nplace - 1)
    if npeers:
        barrier = pltpu.get_barrier_semaphore()

        def greet_frame(k):
            pl.semaphore_signal(
                barrier, inc=1, device_id={"frame": lax.rem(me + k, nf)}, device_id_type=MESH
            )

        def greet_place(k):
            where = lax.rem(place + 1 + k // max(pair, 1), nplace)
            frame = lax.rem(k, max(pair, 1)) * 2 + lax.rem(me, 2)
            pl.semaphore_signal(barrier, inc=1, device_id=there(frame, where), device_id_type=MESH)

        loop(1, nf, greet_frame)
        loop(0, max(pair, 1) * (nplace - 1), greet_place)

    coefs[...] = jnp.zeros((ITEMS, 128), F32)
    bent[...] = jnp.zeros((ITEMS * 16, 128), F32)
    for f in range(FRAMES):
        for s in range(FIELDS):
            coefs[pl.ds(s * 4 + f, 1), pl.ds(0, MODES)] = coefs_in[f, s // 2, pl.ds(s % 2, 1), :]

    rows64 = lax.broadcasted_iota(jnp.int32, (HALF, 128), 0).astype(F32)
    cols8 = lanes.astype(F32)

    def data_field(s):
        r, c_ = s // 2, lax.rem(s, 2)
        kind = kinds[r, c_]
        window = jnp.where(
            kind == 0, taper[pl.ds(0, 1), :],
            jnp.where(
                kind == 1, taper[pl.ds(1, 1), :],
                jnp.where(kind == 2, taper[pl.ds(2, 1), :], taper[pl.ds(3, 1), :]),
            ),
        )
        rotor = jnp.concatenate(two(qd[...] * window), axis=1)
        both = jnp.concatenate([window, window], axis=1)
        ready = []
        middle = []
        turns = []
        for f in range(FRAMES):
            c0 = corners[0, r, c_, f].astype(F32)
            c1 = corners[1, r, c_, f].astype(F32)
            image = jnp.concatenate([images[f, r, c_, 0], images[f, r, c_, 1]], axis=1)
            lines = jnp.dot(
                rotor, jnp.concatenate([image, image], axis=0), preferred_element_type=F32
            )
            lines = lines * both
            cycles = rows64 * (c0 * np.float32(1.0 / PIXELS))
            cycles = cycles - jnp.floor(cycles + 0.5)
            rs, rc = sincos(cycles * np.float32(2.0 * math.pi))
            cycles = cols8 * (c1 * np.float32(1.0 / PIXELS))
            cycles = cycles - jnp.floor(cycles + 0.5)
            cs, cc = sincos(cycles * np.float32(2.0 * math.pi))
            turns.append((cs[:1] * np.float32(1.0 / PIXELS), cc[:1] * np.float32(1.0 / PIXELS)))
            c0h = c0 * 0.5
            alternate = (1.0 - 4.0 * jnp.abs(c0h - jnp.floor(c0h))) * np.float32(1.0 / PIXELS)
            for c in range(2):
                zr = lines[:64, c * 128 : c * 128 + 128]
                zi = lines[64:, c * 128 : c * 128 + 128]
                middle.append(jnp.sum(zi[:1], axis=1, keepdims=True) * alternate)
                zi = patched(zi, jnp.where(subs == 0, 0.0, zi[:8]))
                ready.append(jnp.concatenate([zr * rc - zi * rs, zr * rs + zi * rc], axis=1))
        spec = right(jnp.concatenate(ready, axis=0), w4[...])
        for f in range(FRAMES):
            cs, cc = turns[f]
            for c in range(2):
                at = (f * 2 + c) * 64
                dr = spec[at : at + 64, :128]
                di = spec[at : at + 64, 128:]
                data[s * 4 + f, pl.ds(c * 64, 64), pl.ds(0, 128)] = dr * cc - di * cs
                di = dr * cs + di * cc
                data[s * 4 + f, pl.ds(c * 64, 64), pl.ds(128, 128)] = patched(
                    di, jnp.where(m00, middle[f * 2 + c], di[:8])
                )

    loop(0, FIELDS, data_field)

    if npeers:
        pl.semaphore_wait(barrier, npeers)

    def remote(src, dst, send, recv, device):
        return pltpu.make_async_remote_copy(
            src_ref=src, dst_ref=dst, send_sem=send, recv_sem=recv,
            device_id=device, device_id_type=MESH,
        )

    def owner(s, k):
        return lax.rem(s, 2) * owners + k

    def rs_copy(it, s, k, slot):
        return remote(
            sums.at[it, s, pl.ds(k * own, own)], parts.at[it, s // 2, slot],
            rs_send.at[it, s, k], rs_recv.at[it, s // 2, slot], {"frame": owner(s, k)},
        )

    def send_field(it, s):
        if nf > 1:
            def act(k):
                pl.when(owner(s, k) != me)(lambda: rs_copy(it, s, k, me).start())

            loop(0, owners, act)

    def rs_arrival(it, s, peer):
        return remote(
            sums.at[it, s, pl.ds(0, own)], parts.at[it, s // 2, peer],
            rs_send.at[it, s, 0], rs_recv.at[it, s // 2, peer], {"frame": peer},
        )

    def ag_copy(it, s, k, peer):
        at = pl.ds(k * own, own)
        return remote(
            objs.at[it, s, at], objs.at[it, s, at],
            ag_send.at[it, s // 2, peer], ag_recv.at[it, s, k], {"frame": peer},
        )

    def mine(s):
        return me // owners == lax.rem(s, 2) if nf > 1 else s >= 0

    def reduce_field(it, s):
        @pl.when(mine(s))
        def _():
            k = lax.rem(me, owners)
            loop(1, nf, lambda j: rs_arrival(it, s, lax.rem(me + j, nf)).wait_recv())
            for j in range(own):
                tile = k * own + j
                total = sums[it, s, tile]
                for other in range(1, nf):
                    total = total + parts[it, s // 2, lax.rem(me + other, nf), j]
                first = tile == 0
                real, imag, power = total[0], total[1], total[2]
                n = noise[0, 0]
                other = jnp.where(m00 & first, pltpu.roll(imag, 64, 1), power)
                objs[it, s, tile, 0] = real / (power + n)
                objs[it, s, tile, 1] = jnp.where(m064 & first, 0.0, imag / (other + n))
            loop(1, nf, lambda j: ag_copy(it, s, k, lax.rem(me + j, nf)).start())

    def wait_field(it, s):
        if nf > 1:
            def act(k):
                peer = owner(s, k)
                pl.when(peer != me)(lambda: ag_copy(it, s, k, peer).wait_recv())

            loop(0, owners, act)

    def n1_copy(it, slot):
        return remote(
            norm1.at[it, lax.rem(me, 2)], norm1.at[it, slot],
            n1_send.at[it], n1_recv.at[it], {"frame": me + 1 - 2 * lax.rem(me, 2)},
        )

    def n2_copy(it, k):
        frame, where = chip_at(k)
        slot = me // 2 * nplace + place
        return remote(
            norm2.at[it, slot], norm2.at[it, slot],
            n2_send.at[it], n2_recv.at[it], there(frame, where),
        )

    def halo_copies(it):
        def one(axis, index, count, delta, slot):
            peer = jnp.clip(index + delta, 0, count - 1)
            inside = (index + delta >= 0) & (index + delta < count)
            return inside, remote(
                halo.at[it, 4], halo.at[it, slot], h_send.at[it, slot], h_recv.at[it, slot], {axis: peer}
            )

        out = []
        if nr > 1:
            out += [one("row", row, nr, 1, 0), one("row", row, nr, -1, 1)]
        if nc > 1:
            out += [one("col", col, nc, 1, 2), one("col", col, nc, -1, 3)]
        return out

    def halo_sides():
        out = []
        if nr > 1:
            out += [(0, row > 0), (1, row < nr - 1)]
        if nc > 1:
            out += [(2, col > 0), (3, col < nc - 1)]
        return out

    def forward(it, s):
        stacks = []
        for f in range(FRAMES):
            x = bent[pl.ds(pl.multiple_of((s * 4 + f) * 16, 16), 16), :]
            h, m, l = three(x)
            stacks.append(jnp.concatenate([h, m, h, l, h, m], axis=0))
        phases = jnp.dot(y1[...], jnp.concatenate(stacks, axis=1), preferred_element_type=F32)
        mask = lens[0]
        none = jnp.zeros((PAD - SIDE, 256), F32)
        pupil = []
        for f in range(FRAMES):
            item = s * 4 + f
            sin0, cos0 = sincos(phases[:, f * 128 : f * 128 + 128])
            cos0 = cos0 * mask
            sin0 = sin0 * mask
            cos1 = cos0 * lens[1] - sin0 * lens[2]
            sin1 = sin0 * lens[1] + cos0 * lens[2]
            fields[item, 0] = cos0
            fields[item, 1] = sin0
            fields[item, 2] = cos1
            fields[item, 3] = sin1
            pupil += [
                jnp.concatenate([cos0, sin0], axis=1), none,
                jnp.concatenate([cos1, sin1], axis=1), none,
            ]
        lines = right(jnp.concatenate(pupil, axis=0), w1[...])
        z = []
        for f in range(FRAMES):
            evens = []
            odds = []
            for c in range(2):
                at = (f * 2 + c) * PAD
                wave = left(l2[...], lines[at : at + PAD])
                waves[s * 4 + f, c] = wave
                a, b = wave[:64, :128], wave[:64, 128:]
                e, d = wave[64:, :128], wave[64:, 128:]
                ab = a * a + b * b
                ed = e * e + d * d
                even = ab + ed
                odd = 2.0 * (a * d - b * e)
                evens.append(patched(even, jnp.where(subs == 0, ab[:8], even[:8])))
                odds.append(patched(odd, jnp.where(subs == 0, ed[:8], odd[:8])))
            spread = jnp.concatenate(
                [jnp.concatenate(evens, axis=1), jnp.concatenate(odds, axis=1)], axis=0
            )
            half = left(q[...], spread)
            for c in range(2):
                at = slice(c * 128, c * 128 + 128)
                z.append(jnp.concatenate([half[:64, at], half[64:, at]], axis=1))
        z = right(jnp.concatenate(z, axis=0), w4[...])
        for f in range(FRAMES):
            otf[s * 4 + f] = z[f * 128 : f * 128 + 128]
        for t in range(TILES):
            cr = ci = pw = None
            for f in range(FRAMES):
                for c in range(2):
                    at = f * 128 + c * 64 + t * 8
                    zr, zi = z[at : at + 8, :128], z[at : at + 8, 128:]
                    dr = data[s * 4 + f, pl.ds(c * 64 + t * 8, 8), pl.ds(0, 128)]
                    di = data[s * 4 + f, pl.ds(c * 64 + t * 8, 8), pl.ds(128, 128)]
                    ii = zi * di
                    zz = zi * zi
                    im = zr * di - zi * dr
                    if t == 0:
                        im = jnp.where(m00, ii, im)
                        im = jnp.where(m064, pltpu.roll(zz, 64, 1), im)
                        ii = jnp.where(m00, 0.0, ii)
                        zz = jnp.where(m00, 0.0, zz)
                    re = zr * dr + ii
                    p = zr * zr + zz
                    cr = re if cr is None else cr + re
                    ci = im if ci is None else ci + im
                    pw = p if pw is None else pw + p
            sums[it, s, t, 0] = cr
            sums[it, s, t, 1] = ci
            sums[it, s, t, 2] = pw

    def backward(it, s):
        res = [[] for _ in range(2 * FRAMES)]
        for t in range(TILES):
            our = objs[it, s, t, 0]
            oui = objs[it, s, t, 1]
            for f in range(FRAMES):
                for c in range(2):
                    at = pl.ds(c * 64 + t * 8, 8)
                    item = s * 4 + f
                    zr, zi = otf[item, at, pl.ds(0, 128)], otf[item, at, pl.ds(128, 128)]
                    dr, di = data[item, at, pl.ds(0, 128)], data[item, at, pl.ds(128, 128)]
                    ii = oui * zi
                    ri = oui * zr
                    rr = our * zi
                    if t == 0:
                        rr = jnp.where(m00, ii, rr)
                        ri = jnp.where(m00, 0.0, ri)
                        ii = jnp.where(m00, 0.0, ii)
                    er = dr - (our * zr - ii)
                    ei = di - (rr + ri)
                    x = ei * oui
                    y = ei * our
                    w = er * oui
                    if t == 0:
                        y = jnp.where(m00, x, y)
                        x = jnp.where(m00, 0.0, x)
                        w = jnp.where(m00, 0.0, w)
                    res[f * 2 + c].append(jnp.concatenate([er * our + x, y - w], axis=1))
        dz = right(jnp.concatenate(sum(res, []), axis=0), w4t[...])
        dlines = []
        zero = subs == 0
        for f in range(FRAMES):
            at = f * 128
            half = jnp.concatenate(
                [
                    jnp.concatenate([dz[at : at + 64, :128], dz[at + 64 : at + 128, :128]], axis=1),
                    jnp.concatenate([dz[at : at + 64, 128:], dz[at + 64 : at + 128, 128:]], axis=1),
                ],
                axis=0,
            )
            dspread = left(qt[...], half)
            for c in range(2):
                de = dspread[:64, c * 128 : c * 128 + 128]
                do = dspread[64:, c * 128 : c * 128 + 128]
                wave = waves[s * 4 + f, c]
                a, b = wave[:64, :128], wave[:64, 128:]
                e, d = wave[64:, :128], wave[64:, 128:]
                da = a * de + d * do
                db = b * de - e * do
                dc = e * de - b * do
                dd = d * de + a * do
                de8, do8 = de[:8], do[:8]
                da = patched(da, jnp.where(zero, a[:8] * de8, da[:8]))
                db = patched(db, jnp.where(zero, b[:8] * de8, db[:8]))
                dc = patched(dc, jnp.where(zero, e[:8] * do8, dc[:8]))
                dd = patched(dd, jnp.where(zero, d[:8] * do8, dd[:8]))
                dwave = jnp.concatenate(
                    [jnp.concatenate([da, db], axis=1), jnp.concatenate([dc, dd], axis=1)], axis=0
                )
                dlines.append(left(l2t[...], dwave))
        dpupil = right(jnp.concatenate(dlines, axis=0), w1t[...])
        dphase = []
        for f in range(FRAMES):
            total = None
            for c in range(2):
                at = (f * 2 + c) * PAD
                part = (
                    fields[s * 4 + f, 2 * c] * dpupil[at : at + SIDE, 128:]
                    - fields[s * 4 + f, 2 * c + 1] * dpupil[at : at + SIDE, :128]
                )
                total = part if total is None else total + part
            dphase.append(total)
        dphase = jnp.concatenate(dphase, axis=1)
        dphase = jnp.concatenate([dphase, jnp.zeros((PAD - SIDE, FRAMES * 128), F32)], axis=0)
        out = left(y2[...], dphase)
        for f in range(FRAMES):
            dbent[pl.ds(pl.multiple_of((s * 4 + f) * 16, 16), 16), :] = out[:, f * 128 : f * 128 + 128]

    def iteration(it):
        halo[it, 4] = coefs[...]
        for inside, copy in halo_copies(it):
            pl.when(inside)(copy.start)

        cf = coefs[...]
        ch = cf.astype(BF16).astype(F32)
        cm = (cf - ch).astype(BF16).astype(F32)
        cl = (cf - ch - cm).astype(BF16).astype(F32)
        low = ch + pltpu.roll(cm, 36, 1) + pltpu.roll(ch, 72, 1)
        high = cl + pltpu.roll(ch, 36, 1) + pltpu.roll(cm, 72, 1)
        lhs = jnp.concatenate([low, high], axis=1).astype(BF16)
        out = jnp.dot(lhs, t1[...], preferred_element_type=F32)
        for i in range(DEGREE):
            bent[pl.ds(i, ITEMS, stride=16), :] = out[:, i * 128 : i * 128 + 128]

        def forward_step(s):
            forward(it, s)
            send_field(it, s)
            pl.when(s >= 2)(lambda: reduce_field(it, s - 2))

        def backward_step(s):
            pl.when(s < 2)(lambda: reduce_field(it, s + 2))
            wait_field(it, s)
            backward(it, s)

        loop(0, FIELDS, forward_step)
        loop(0, FIELDS, backward_step)

        x = jnp.concatenate([dbent[pl.ds(i, ITEMS, stride=16), :] for i in range(DEGREE)], axis=1)
        acc = jnp.dot(jnp.concatenate(two(x), axis=0), t2[...], preferred_element_type=F32)
        grads = acc[:16] + pltpu.roll(acc[:16], 64, 1) + acc[16:]
        lane16 = lax.broadcasted_iota(jnp.int32, (ITEMS, 128), 1)
        grads = jnp.where(lane16 < MODES, grads, 0.0)

        sq = grads * grads
        total = jnp.sum(sq[:8] + sq[8:], axis=0, keepdims=True)
        slot = me // 2 * nplace + place
        if nf > 1:
            norm1[it, lax.rem(me, 2)] = total
            n1_copy(it, lax.rem(me, 2)).start()
            n1_copy(it, 1 - lax.rem(me, 2)).wait_recv()
            total = norm1[it, 0] + norm1[it, 1]
        norm2[it, slot] = total
        loop(1, chips, lambda k: n2_copy(it, k).start())

        for side, inside in halo_sides():
            @pl.when(inside)
            def _(side=side):
                pltpu.make_async_copy(halo.at[it, side], halo.at[it, side], h_recv.at[it, side]).wait()

        above, below = halo[it, 0, 8:], halo[it, 1, :8]
        laplace = []
        for r in range(2):
            mine_ = cf[r * 8 : r * 8 + 8]
            other = cf[8 - r * 8 : 16 - r * 8]
            beside = jnp.where(
                subs < 4,
                pltpu.roll(halo[it, 2, r * 8 : r * 8 + 8], 4, 0),
                pltpu.roll(halo[it, 3, r * 8 : r * 8 + 8], 4, 0),
            )
            out = 4.0 * mine_ - other - pltpu.roll(mine_, 4, 0) - beside
            laplace.append(out - (above if r == 0 else below))
        laplace = jnp.concatenate(laplace, axis=0)

        if chips > 1:
            rest = pl.ds(0, chips - 1)
            pltpu.make_async_copy(norm2.at[it, rest], norm2.at[it, rest], n2_recv.at[it]).wait()
        total = jnp.sum(jnp.sum(norm2[it], axis=0), axis=1, keepdims=True)
        count = ITEMS * MODES * nf * nplace
        scale = jnp.sqrt(total / count + TINY)
        coefs[...] = cf - step[0, 0] * (grads / scale + smooth[0, 0] * laplace)

    def departures(it):
        if nf > 1:
            def field(s):
                def act(k):
                    pl.when(owner(s, k) != me)(lambda: rs_copy(it, s, k, me).wait_send())

                loop(0, owners, act)

                @pl.when(mine(s))
                def _():
                    k = lax.rem(me, owners)
                    loop(1, nf, lambda j: ag_copy(it, s, k, lax.rem(me + j, nf)).wait_send())

            loop(0, FIELDS, field)
            n1_copy(it, lax.rem(me, 2)).wait_send()
        if chips > 1:
            rest = pl.ds(0, chips - 1)
            pltpu.make_async_copy(norm2.at[it, rest], norm2.at[it, rest], n2_send.at[it]).wait()
        for inside, copy in halo_copies(it):
            pl.when(inside)(copy.wait_send)

    loop(0, ITERS, iteration)

    for f in range(FRAMES):
        for s in range(FIELDS):
            coefs_out[f, s // 2, pl.ds(s % 2, 1), :] = coefs[pl.ds(s * 4 + f, 1), pl.ds(0, MODES)]

    last = ITERS - 1
    for j in range(per):
        tile = me * per + j

        @pl.when(tile < 8)
        def _(j=j, tile=tile):
            for s in range(FIELDS):
                re = objs[last, s, tile, 0]
                im = objs[last, s, tile, 1]
                object_out[0, s // 2, s % 2, pl.ds(j * 8, 8), :] = re
                object_out[1, s // 2, s % 2, pl.ds(j * 8, 8), :] = jnp.where(m00 & (tile == 0), 0.0, im)

        @pl.when(tile >= 8)
        def _(j=j, tile=tile):
            g = tile - 8
            for s in range(FIELDS):
                for c in range(2):
                    at = (s * 2 + c) * 8
                    for i in range(1, 8):
                        turned[pl.ds(at + i, 1), :] = objs[last, s, 7 - g, c, pl.ds(8 - i, 1), :]
                    zero = objs[last, s, lax.rem(8 - g, 8), c, pl.ds(0, 1), :]
                    if c == 0:
                        middle = objs[last, s, 0, 1, pl.ds(0, 1), :]
                        middle = jnp.where(lanes[:1] == 0, middle, 0.0)
                    else:
                        middle = jnp.zeros((1, 128), F32)
                    turned[pl.ds(at, 1), :] = jnp.where(g == 0, middle, zero)
            out = jnp.dot(
                jnp.concatenate(three(turned[...]), axis=1), flip[...], preferred_element_type=F32
            )
            for s in range(FIELDS):
                at = s * 16
                object_out[0, s // 2, s % 2, pl.ds(j * 8, 8), :] = out[at : at + 8]
                object_out[1, s // 2, s % 2, pl.ds(j * 8, 8), :] = -out[at + 8 : at + 16]

    loop(0, ITERS, departures)


def solution(mesh):
    nf, nr, nc = (mesh.shape[name] for name in ("frame", "row", "col"))
    host = tables()
    per = 16 // nf
    vmem = pl.BlockSpec(memory_space=pltpu.VMEM)
    smem = pl.BlockSpec(memory_space=pltpu.SMEM)

    def body(images, corners, kinds, coefs, step, noise, smooth):
        own = min(per, TILES)
        chips = max(nf // 2, 1) * nr * nc
        scratch = [
            pltpu.VMEM((ITEMS, 128), F32),
            pltpu.VMEM((ITERS, 5, ITEMS, 128), F32),
            pltpu.VMEM((ITEMS * 16, 128), F32),
            pltpu.VMEM((ITEMS * 16, 128), F32),
            pltpu.VMEM((ITEMS, 4, SIDE, 128), F32),
            pltpu.VMEM((ITEMS, 2, 128, 256), F32),
            pltpu.VMEM((ITEMS, 128, 256), F32),
            pltpu.VMEM((ITEMS, 128, 256), F32),
            pltpu.VMEM((ITERS, FIELDS, TILES, 3, 8, 128), F32),
            pltpu.VMEM((ITERS, 2, nf, own, 3, 8, 128), F32),
            pltpu.VMEM((ITERS, FIELDS, TILES, 2, 8, 128), F32),
            pltpu.VMEM((ITERS, 2, 1, 128), F32),
            pltpu.VMEM((ITERS, chips, 1, 128), F32),
            pltpu.VMEM((HALF, 128), F32),
        ]
        dma = pltpu.SemaphoreType.DMA
        scratch += [dma((ITERS, FIELDS, TILES)), dma((ITERS, 2, nf))]
        scratch += [dma((ITERS, 2, nf)), dma((ITERS, FIELDS, TILES))]
        scratch += [dma((ITERS,)) for _ in range(4)]
        scratch += [dma((ITERS, 4)) for _ in range(2)]
        single = lambda x: x.reshape(1, 1)
        return pl.pallas_call(
            functools.partial(kernel, nf, nr, nc),
            out_shape=(
                jax.ShapeDtypeStruct((FRAMES, 2, 2, MODES), F32),
                jax.ShapeDtypeStruct((2, 2, 2, 8 * per, 128), F32),
            ),
            in_specs=[vmem, smem, smem, vmem, smem, smem, smem] + [vmem] * len(NAMES),
            out_specs=(vmem, vmem),
            scratch_shapes=scratch,
            compiler_params=pltpu.CompilerParams(
                collective_id=0 if nf * nr * nc > 1 else None,
                has_side_effects=True,
                vmem_limit_bytes=56 * 1024 * 1024,
            ),
        )(
            images, corners.transpose(0, 2, 3, 1), kinds, coefs, single(step), single(noise), single(smooth),
            *[jnp.asarray(host[name]) for name in NAMES],
        )

    in_specs = (
        P("frame", "row", "col", None, None, None),
        P(None, "frame", "row", "col"),
        P("row", "col"),
        P("frame", "row", "col", None),
        P(),
        P(),
        P(),
    )
    out_specs = (P("frame", "row", "col", None), P(None, "row", "col", "frame", None))
    return jax.shard_map(body, mesh=mesh, in_specs=in_specs, out_specs=out_specs, check_vma=False)
```

time: 130 us -> 82.9 us (0.64)
  Pallas kernels: 123 us -> 77.4 us
  local copies, waits for them, and re-layouts: 4.05 us -> 2.67 us
    pallas_call x1, Pallas kernels: 123 us -> 77.4 us  [body(): pl.pallas_call(functools.partial(kernel, nf, nr, nc), out_shape=(jax.Shap...]
    unnamed x3 -> x2, local copies, waits for them, and re-layouts: 4.05 us -> 2.67 us
where the time goes in v2:
time: 82.9 us; the launch traced here: 82.7 us
  Pallas kernels  77.4 us (93%)
  local copies, waits for them, and re-layouts  2.67 us (3%)
  between operations  2.58 us (3%)
    pallas_call x1, Pallas kernels, body(): pl.pallas_call(functools.partial(kernel, nf, nr, nc), out_shape=(jax.Shap...  77.4 us
    unnamed x2, local copies, waits for them, and re-layouts  2.67 us

profile of v2, /device:TPU:1, one launch (start us, length us, event | category | flops | bytes accessed | tf_op | source)
XLA Modules:
  0.0 82.7 jit_solution(2766065537748440326)
XLA Ops:
  2.6 77.4 %shard_map.230 = (f32[4,2,2,36]{3,2,1,0:T(2,128)}, f32[2,2,2,8,128]{4,3,2,1,0:T(8,128)}) custom-call(bf16[4,2,2,2,128,128]{5,4,3,2,1,0:T(8,128)(2,1)} %images.1, s32[2,2,2,4]{3,2,1,0:T(2,128)} %bitcast.7, s32[2,2]{1,0:T(2,128)} %kinds.1, f32[4,2,2,36]{3,2,1,0:T(2,128)} %coefs_in.1, f32[1,1]{1,0:T(1,128)} %bitcast.4.step, f32[1,1]{1,0:T(1,128)} %bitcast.5.noise, ...), custom_call_target="tpu_custom_call" | custom-call | tf_op jit(solution)/shard_map/pallas_call | solution.py:805
  80.0 1.3 %copy.30 = f32[4,2,2,36]{3,2,1,0:T(2,128)} copy(f32[4,2,2,36]{3,2,1,0:T(2,128)} %get-tuple-element.4) | data formatting | bytes 4608
  81.3 1.4 %copy.31 = f32[2,2,2,8,128]{4,3,2,1,0:T(8,128)} copy(f32[2,2,2,8,128]{4,3,2,1,0:T(8,128)} %get-tuple-element.5) | data formatting | bytes 65536

commit v3 on v2

--- a/solution.py
+++ b/solution.py
@@ -12,7 +12,10 @@
 
 ITERS = 2
 MODES = 36
+SKEW = 3
+GROUP = 2
 DEGREE = 9
+TERMS = DEGREE + 1
 DIVERSITY = 1.5
 TINY = 1e-06
 PIXELS = 128
@@ -93,18 +96,23 @@
     half = np.arange(HALF)
     pupil = np.arange(-RADIUS, RADIUS + 1)
 
-    ang = turn * (pupil[:, None] * freq[None, :] % PIXELS)
-    w1 = np.zeros((256, 256))
-    w1[:65, :128] = np.cos(ang)
-    w1[:65, 128:] = -np.sin(ang)
-    w1[128 : 128 + 65, :128] = np.sin(ang)
-    w1[128 : 128 + 65, 128:] = np.cos(ang)
+    ang = turn * (pupil[:64, None] * freq[None, :] % PIXELS)
+    w1 = np.zeros((128, 256))
+    w1[:64, :128] = np.cos(ang)
+    w1[:64, 128:] = -np.sin(ang)
+    w1[64:, :128] = np.sin(ang)
+    w1[64:, 128:] = np.cos(ang)
+    hi, lo = pieces(w1.T, 2)
+    w1t = np.concatenate([np.concatenate([hi, lo], 1), np.concatenate([hi, 0 * lo], 1)], 0)
+    turn65 = np.ones((8, 256), np.float32)
+    turn65[1, :128] = turn65[1, 128:] = (-1.0) ** freq
 
     l2 = np.zeros((128, PAD))
     ang = turn * (half[:, None] * pupil[None, :] % PIXELS)
     l2[:64, :65] = np.cos(ang)
     l2[64:, :65] = np.sin(ang)
     l2[64, :65] = np.cos(turn * (64 * pupil % PIXELS))
+    l2[:, 65] = l2[:, 32]
 
     ang = turn * (half[:, None] * half[None, :] % PIXELS)
     q = np.zeros((128, 128))
@@ -137,28 +145,44 @@
     w4[128:, 128:] = np.cos(ang)
 
     rows_table = np.polynomial.legendre.legvander(pupil / RADIUS, DEGREE - 1)
-    t = np.zeros((MODES, DEGREE, 128))
-    t[:, :, :65] = np.einsum("ip,kpx->kix", np.linalg.pinv(rows_table), modes)
+    t = np.zeros((MODES, TERMS, 128))
+    t[:, :DEGREE, :64] = np.einsum("ip,kpx->kix", np.linalg.pinv(rows_table), modes)[:, :, :64]
+    t[:, DEGREE, 0] = modes[:, 32, 64]
+    t[:, :, 64:] = t[:, :, :64]
     th, tm, tl = pieces(t, 3)
-    t1 = np.zeros((256, DEGREE * 128), ml_dtypes.bfloat16)
+    t1 = np.zeros((256, TERMS * 128), ml_dtypes.bfloat16)
     for at, part in ((0, th), (36, th), (72, tm), (128, th), (164, tl), (200, tm)):
         t1[at : at + MODES] = part.reshape(MODES, -1)
-    t2 = np.zeros((DEGREE * 128, 128), ml_dtypes.bfloat16)
+    t[:, :, :64] *= -1.0
+    th, tm = pieces(t, 2)
+    t2 = np.zeros((TERMS * 128, 128), ml_dtypes.bfloat16)
     t2[:, :MODES] = th.reshape(MODES, -1).T
     t2[:, 64 : 64 + MODES] = tm.reshape(MODES, -1).T
 
     y = np.zeros((SIDE, 16))
     y[:65, :DEGREE] = rows_table
+    y[65, DEGREE] = 1.0
     yh, ym, yl = pieces(y, 3)
     y1 = np.concatenate([yh, yh, ym, yh, yl, ym], axis=1)
     y = np.zeros((16, PAD))
     y[:DEGREE, :65] = rows_table.T
+    y[DEGREE, 65] = 1.0
     y2 = left_table(y)
 
-    lens = np.zeros((3, SIDE, 128), np.float32)
-    lens[0, :65, :65] = mask
-    lens[1, :65, :65] = np.cos(DIVERSITY * modes[2] * mask)
-    lens[2, :65, :65] = np.sin(DIVERSITY * modes[2] * mask)
+    def packed(values, other):
+        out = np.zeros((SIDE, 128))
+        out[:65, :64] = values[:, :64]
+        out[65, 0] = values[32, 64]
+        out[:, 64:] = other * out[:, :64]
+        return out
+
+    lens = np.stack(
+        [
+            packed(mask, 1.0),
+            packed(np.cos(DIVERSITY * modes[2] * mask), 1.0),
+            packed(-np.sin(DIVERSITY * modes[2] * mask), -1.0),
+        ]
+    ).astype(np.float32)
 
     edges = np.minimum(freq, PIXELS - 1 - freq)
     taper = np.zeros((8, 128), np.float32)
@@ -174,7 +198,8 @@
 
     return dict(
         w1=right_table(w1),
-        w1t=right_table(w1.T),
+        w1t=w1t,
+        turn65=turn65,
         l2=left_table(l2),
         l2t=left_table(l2.T),
         q=left_table(q),
@@ -193,7 +218,7 @@
 
 
 NAMES = (
-    "w1", "w1t", "l2", "l2t", "q", "qt", "w4", "w4t", "qd", "t1", "t2", "y1", "y2", "lens", "taper", "flip",
+    "w1", "w1t", "turn65", "l2", "l2t", "q", "qt", "w4", "w4t", "qd", "t1", "t2", "y1", "y2", "lens", "taper", "flip",
 )
 
 
@@ -226,6 +251,19 @@
     return s, c_ * sign
 
 
+def cosine(x):
+    k = jnp.floor(x * np.float32(1.0 / math.pi) + 0.5)
+    r = x - k * np.float32(3.140625)
+    r = r - k * np.float32(0.0009670257568359375)
+    r = r - k * np.float32(6.2771141529083251953e-7)
+    sign = 1.0 - 2.0 * (k - 2.0 * jnp.floor(k * 0.5))
+    r2 = r * r
+    out = np.float32(-2.6e-7)
+    for c in (2.4771e-5, -1.38888e-3, 4.16666e-2, -0.5, 1.0):
+        out = out * r2 + np.float32(c)
+    return out * sign
+
+
 def two(x):
     hi = x.astype(BF16)
     return hi, (x - hi.astype(F32)).astype(BF16)
@@ -248,6 +286,16 @@
     return jnp.dot(table, jnp.concatenate([hi, hi, lo], axis=0), preferred_element_type=F32)
 
 
+def skewed(count, ahead, first, second):
+    waiting = []
+    for i in range(count):
+        waiting.append(first(i))
+        if len(waiting) > ahead:
+            second(waiting.pop(0))
+    for x in waiting:
+        second(x)
+
+
 def patched(whole, first):
     return jnp.concatenate([first, whole[8:]], axis=0)
 
@@ -255,7 +303,7 @@
 def kernel(
     nf, nr, nc,
     images, corners, kinds, coefs_in, step, noise, smooth,
-    w1, w1t, l2, l2t, q, qt, w4, w4t, qd, t1, t2, y1, y2, lens, taper, flip,
+    w1, w1t, turn65, l2, l2t, q, qt, w4, w4t, qd, t1, t2, y1, y2, lens, taper, flip,
     coefs_out, object_out,
     coefs, halo, bent, dbent, fields, waves, otf, data, sums, parts, objs, norm1, norm2, turned,
     rs_send, rs_recv, ag_send, ag_recv, n1_send, n1_recv, n2_send, n2_recv, h_send, h_recv,
@@ -373,9 +421,6 @@
 
     loop(0, FIELDS, data_field)
 
-    if npeers:
-        pl.semaphore_wait(barrier, npeers)
-
     def remote(src, dst, send, recv, device):
         return pltpu.make_async_remote_copy(
             src_ref=src, dst_ref=dst, send_sem=send, recv_sem=recv,
@@ -484,32 +529,38 @@
             h, m, l = three(x)
             stacks.append(jnp.concatenate([h, m, h, l, h, m], axis=0))
         phases = jnp.dot(y1[...], jnp.concatenate(stacks, axis=1), preferred_element_type=F32)
-        mask = lens[0]
-        none = jnp.zeros((PAD - SIDE, 256), F32)
-        pupil = []
-        for f in range(FRAMES):
-            item = s * 4 + f
-            sin0, cos0 = sincos(phases[:, f * 128 : f * 128 + 128])
-            cos0 = cos0 * mask
-            sin0 = sin0 * mask
-            cos1 = cos0 * lens[1] - sin0 * lens[2]
-            sin1 = sin0 * lens[1] + cos0 * lens[2]
-            fields[item, 0] = cos0
-            fields[item, 1] = sin0
-            fields[item, 2] = cos1
-            fields[item, 3] = sin1
-            pupil += [
-                jnp.concatenate([cos0, sin0], axis=1), none,
-                jnp.concatenate([cos1, sin1], axis=1), none,
-            ]
-        lines = right(jnp.concatenate(pupil, axis=0), w1[...])
+        quarter = jnp.where(lanes[:1] < 64, 0.0, np.float32(0.5 * math.pi))
+        none = jnp.zeros((PAD - SIDE, 128), F32)
+        lines = []
+        for g in range(0, FRAMES, GROUP):
+            pupil = []
+            for f in range(g, g + GROUP):
+                item = s * 4 + f
+                one0 = cosine(phases[:, f * 128 : f * 128 + 128] - quarter) * lens[0]
+                two0 = pltpu.roll(one0, 64, 1)
+                one1 = one0 * lens[1] + two0 * lens[2]
+                fields[item, 0] = two0
+                fields[item, 1] = two0 * lens[1] - one0 * lens[2]
+                pupil += [one0, none, one1, none]
+            lines.append(right(jnp.concatenate(pupil, axis=0), w1[...]))
+        lines = jnp.concatenate(lines, axis=0)
         z = []
-        for f in range(FRAMES):
+
+        def first(f):
             evens = []
             odds = []
             for c in range(2):
                 at = (f * 2 + c) * PAD
-                wave = left(l2[...], lines[at : at + PAD])
+                wave = left(
+                    l2[...],
+                    jnp.concatenate(
+                        [
+                            lines[at : at + 64], lines[at + 64 : at + 72] * turn65[...],
+                            lines[at + 72 : at + 80],
+                        ],
+                        axis=0,
+                    ),
+                )
                 waves[s * 4 + f, c] = wave
                 a, b = wave[:64, :128], wave[:64, 128:]
                 e, d = wave[64:, :128], wave[64:, 128:]
@@ -519,14 +570,23 @@
                 odd = 2.0 * (a * d - b * e)
                 evens.append(patched(even, jnp.where(subs == 0, ab[:8], even[:8])))
                 odds.append(patched(odd, jnp.where(subs == 0, ed[:8], odd[:8])))
-            spread = jnp.concatenate(
+            return jnp.concatenate(
                 [jnp.concatenate(evens, axis=1), jnp.concatenate(odds, axis=1)], axis=0
             )
+
+        def second(spread):
             half = left(q[...], spread)
             for c in range(2):
                 at = slice(c * 128, c * 128 + 128)
                 z.append(jnp.concatenate([half[:64, at], half[64:, at]], axis=1))
-        z = right(jnp.concatenate(z, axis=0), w4[...])
+
+        def third():
+            if len(z) % (2 * GROUP) == 0:
+                out.append(right(jnp.concatenate(z[-2 * GROUP :], axis=0), w4[...]))
+
+        out = []
+        skewed(FRAMES, SKEW, first, lambda x: (second(x), third()))
+        z = jnp.concatenate(out, axis=0)
         for f in range(FRAMES):
             otf[s * 4 + f] = z[f * 128 : f * 128 + 128]
         for t in range(TILES):
@@ -555,37 +615,35 @@
             sums[it, s, t, 2] = pw
 
     def backward(it, s):
-        res = [[] for _ in range(2 * FRAMES)]
-        for t in range(TILES):
-            our = objs[it, s, t, 0]
-            oui = objs[it, s, t, 1]
-            for f in range(FRAMES):
-                for c in range(2):
-                    at = pl.ds(c * 64 + t * 8, 8)
-                    item = s * 4 + f
-                    zr, zi = otf[item, at, pl.ds(0, 128)], otf[item, at, pl.ds(128, 128)]
-                    dr, di = data[item, at, pl.ds(0, 128)], data[item, at, pl.ds(128, 128)]
-                    ii = oui * zi
-                    ri = oui * zr
-                    rr = our * zi
-                    if t == 0:
-                        rr = jnp.where(m00, ii, rr)
-                        ri = jnp.where(m00, 0.0, ri)
-                        ii = jnp.where(m00, 0.0, ii)
-                    er = dr - (our * zr - ii)
-                    ei = di - (rr + ri)
-                    x = ei * oui
-                    y = ei * our
-                    w = er * oui
-                    if t == 0:
-                        y = jnp.where(m00, x, y)
-                        x = jnp.where(m00, 0.0, x)
-                        w = jnp.where(m00, 0.0, w)
-                    res[f * 2 + c].append(jnp.concatenate([er * our + x, y - w], axis=1))
-        dz = right(jnp.concatenate(sum(res, []), axis=0), w4t[...])
+        dz = []
+        for g in range(0, FRAMES, GROUP):
+            res = [[] for _ in range(2 * GROUP)]
+            for t in range(TILES):
+                our = objs[it, s, t, 0]
+                oui = objs[it, s, t, 1]
+                oor = ooi = our * our + oui * oui
+                if t == 0:
+                    oor = jnp.where(m00, our * our, oor)
+                    ooi = jnp.where(m00, oui * oui, ooi)
+                for f in range(g, g + GROUP):
+                    for c in range(2):
+                        at = pl.ds(c * 64 + t * 8, 8)
+                        item = s * 4 + f
+                        zr, zi = otf[item, at, pl.ds(0, 128)], otf[item, at, pl.ds(128, 128)]
+                        dr, di = data[item, at, pl.ds(0, 128)], data[item, at, pl.ds(128, 128)]
+                        ii = di * oui
+                        im = di * our - dr * oui
+                        if t == 0:
+                            im = jnp.where(m00, ii, im)
+                            ii = jnp.where(m00, 0.0, ii)
+                        real = dr * our + ii - oor * zr
+                        res[(f - g) * 2 + c].append(jnp.concatenate([real, im - ooi * zi], axis=1))
+            dz.append(right(jnp.concatenate(sum(res, []), axis=0), w4t[...]))
+        dz = jnp.concatenate(dz, axis=0)
         dlines = []
         zero = subs == 0
-        for f in range(FRAMES):
+
+        def first(f):
             at = f * 128
             half = jnp.concatenate(
                 [
@@ -595,6 +653,7 @@
                 axis=0,
             )
             dspread = left(qt[...], half)
+            dwaves = []
             for c in range(2):
                 de = dspread[:64, c * 128 : c * 128 + 128]
                 do = dspread[64:, c * 128 : c * 128 + 128]
@@ -610,22 +669,36 @@
                 db = patched(db, jnp.where(zero, b[:8] * de8, db[:8]))
                 dc = patched(dc, jnp.where(zero, e[:8] * do8, dc[:8]))
                 dd = patched(dd, jnp.where(zero, d[:8] * do8, dd[:8]))
-                dwave = jnp.concatenate(
+                dwaves.append(jnp.concatenate(
                     [jnp.concatenate([da, db], axis=1), jnp.concatenate([dc, dd], axis=1)], axis=0
+                ))
+            return dwaves
+
+        def second(dwaves):
+            for dwave in dwaves:
+                x = left(l2t[...], dwave)
+                dlines.append(
+                    jnp.concatenate([x[:64], x[64:72] * turn65[...], x[72:]], axis=0)
                 )
-                dlines.append(left(l2t[...], dwave))
-        dpupil = right(jnp.concatenate(dlines, axis=0), w1t[...])
+
+        def third():
+            if len(dlines) % (2 * GROUP) == 0:
+                x = jnp.concatenate(dlines[-2 * GROUP :], axis=0)
+                x = jnp.dot(
+                    jnp.concatenate(two(x), axis=1), w1t[...], preferred_element_type=F32
+                )
+                dpupil.append(x[:, :128] + x[:, 128:])
+
+        dpupil = []
+        skewed(FRAMES, SKEW, first, lambda x: (second(x), third()))
+        dpupil = jnp.concatenate(dpupil, axis=0)
         dphase = []
         for f in range(FRAMES):
-            total = None
-            for c in range(2):
-                at = (f * 2 + c) * PAD
-                part = (
-                    fields[s * 4 + f, 2 * c] * dpupil[at : at + SIDE, 128:]
-                    - fields[s * 4 + f, 2 * c + 1] * dpupil[at : at + SIDE, :128]
-                )
-                total = part if total is None else total + part
-            dphase.append(total)
+            at = f * 2 * PAD
+            dphase.append(
+                fields[s * 4 + f, 0] * dpupil[at : at + SIDE]
+                + fields[s * 4 + f, 1] * dpupil[at + PAD : at + PAD + SIDE]
+            )
         dphase = jnp.concatenate(dphase, axis=1)
         dphase = jnp.concatenate([dphase, jnp.zeros((PAD - SIDE, FRAMES * 128), F32)], axis=0)
         out = left(y2[...], dphase)
@@ -633,10 +706,6 @@
             dbent[pl.ds(pl.multiple_of((s * 4 + f) * 16, 16), 16), :] = out[:, f * 128 : f * 128 + 128]
 
     def iteration(it):
-        halo[it, 4] = coefs[...]
-        for inside, copy in halo_copies(it):
-            pl.when(inside)(copy.start)
-
         cf = coefs[...]
         ch = cf.astype(BF16).astype(F32)
         cm = (cf - ch).astype(BF16).astype(F32)
@@ -645,11 +714,13 @@
         high = cl + pltpu.roll(ch, 36, 1) + pltpu.roll(cm, 72, 1)
         lhs = jnp.concatenate([low, high], axis=1).astype(BF16)
         out = jnp.dot(lhs, t1[...], preferred_element_type=F32)
-        for i in range(DEGREE):
+        for i in range(TERMS):
             bent[pl.ds(i, ITEMS, stride=16), :] = out[:, i * 128 : i * 128 + 128]
 
         def forward_step(s):
             forward(it, s)
+            if npeers:
+                pl.when((it == 0) & (s == 0))(lambda: pl.semaphore_wait(barrier, npeers))
             send_field(it, s)
             pl.when(s >= 2)(lambda: reduce_field(it, s - 2))
 
@@ -659,9 +730,14 @@
             backward(it, s)
 
         loop(0, FIELDS, forward_step)
+
+        halo[it, 4] = cf
+        for inside, copy in halo_copies(it):
+            pl.when(inside)(copy.start)
+
         loop(0, FIELDS, backward_step)
 
-        x = jnp.concatenate([dbent[pl.ds(i, ITEMS, stride=16), :] for i in range(DEGREE)], axis=1)
+        x = jnp.concatenate([dbent[pl.ds(i, ITEMS, stride=16), :] for i in range(TERMS)], axis=1)
         acc = jnp.dot(jnp.concatenate(two(x), axis=0), t2[...], preferred_element_type=F32)
         grads = acc[:16] + pltpu.roll(acc[:16], 64, 1) + acc[16:]
         lane16 = lax.broadcasted_iota(jnp.int32, (ITEMS, 128), 1)
@@ -785,7 +861,7 @@
             pltpu.VMEM((ITERS, 5, ITEMS, 128), F32),
             pltpu.VMEM((ITEMS * 16, 128), F32),
             pltpu.VMEM((ITEMS * 16, 128), F32),
-            pltpu.VMEM((ITEMS, 4, SIDE, 128), F32),
+            pltpu.VMEM((ITEMS, 2, SIDE, 128), F32),
             pltpu.VMEM((ITEMS, 2, 128, 256), F32),
             pltpu.VMEM((ITEMS, 128, 256), F32),
             pltpu.VMEM((ITEMS, 128, 256), F32),

time: 82.9 us -> 74.7 us (0.901)
  Pallas kernels: 77.4 us -> 69.2 us
    pallas_call x1, Pallas kernels: 77.4 us -> 69.2 us  [body(): pl.pallas_call(functools.partial(kernel, nf, nr, nc), out_shape=(jax.Shap...]
where the time goes in v3:
time: 74.7 us; the launch traced here: 74.5 us
  Pallas kernels  69.2 us (93%)
  local copies, waits for them, and re-layouts  2.67 us (4%)
  between operations  2.58 us (3%)
    pallas_call x1, Pallas kernels, body(): pl.pallas_call(functools.partial(kernel, nf, nr, nc), out_shape=(jax.Shap...  69.2 us
    unnamed x2, local copies, waits for them, and re-layouts  2.67 us

profile of v3, /device:TPU:1, one launch (start us, length us, event | category | flops | bytes accessed | tf_op | source)
XLA Modules:
  0.0 74.5 jit_solution(11756406239210078071)
XLA Ops:
  2.6 69.2 %shard_map.239 = (f32[4,2,2,36]{3,2,1,0:T(2,128)}, f32[2,2,2,8,128]{4,3,2,1,0:T(8,128)}) custom-call(bf16[4,2,2,2,128,128]{5,4,3,2,1,0:T(8,128)(2,1)} %images.1, s32[2,2,2,4]{3,2,1,0:T(2,128)} %bitcast.7, s32[2,2]{1,0:T(2,128)} %kinds.1, f32[4,2,2,36]{3,2,1,0:T(2,128)} %coefs_in.1, f32[1,1]{1,0:T(1,128)} %bitcast.4.step, f32[1,1]{1,0:T(1,128)} %bitcast.5.noise, ...), custom_call_target="tpu_custom_call" | custom-call | tf_op jit(solution)/shard_map/pallas_call | solution.py:881
  71.8 1.3 %copy.31 = f32[4,2,2,36]{3,2,1,0:T(2,128)} copy(f32[4,2,2,36]{3,2,1,0:T(2,128)} %get-tuple-element.4) | data formatting | bytes 4608
  73.1 1.4 %copy.32 = f32[2,2,2,8,128]{4,3,2,1,0:T(8,128)} copy(f32[2,2,2,8,128]{4,3,2,1,0:T(8,128)} %get-tuple-element.5) | data formatting | bytes 65536

commit v4 on v3

--- a/solution.py
+++ b/solution.py
@@ -334,30 +334,36 @@
 
     halo[...] = jnp.zeros(halo.shape, F32)
 
-    def chip_at(k):
-        mine = me // 2 * nplace + place
-        chip = lax.rem(mine + k, chips)
-        return chip // nplace * 2 + lax.rem(me, 2), lax.rem(chip, nplace)
-
-    def there(frame, where):
-        return {"frame": frame, "row": where // nc, "col": lax.rem(where, nc)}
+    def after(index, step, count):
+        moved = index + step
+        return jnp.where(moved >= count, moved - count, moved)
+
+    frames = [after(me, k, nf) for k in range(nf)]
+    rows = [after(row, k, nr) for k in range(nr)]
+    cols = [after(col, k, nc) for k in range(nc)]
+
+    def far(steps):
+        k, dr, dc = steps
+        dy, dx = k // 2, dc * 2 + k % 2
+        return min(dy, 4 - dy) + min(dr, nr - dr) + min(dx, 4 - dx)
+
+    others = [(k, dr, dc) for k in range(max(pair, 1)) for dr in range(nr) for dc in range(nc)]
+    others = sorted(others, key=far, reverse=True)
+    others = [x for x in others if x != (0, 0, 0)]
+
+    def there(steps):
+        k, dr, dc = steps
+        return {"frame": frames[2 * k], "row": rows[dr], "col": cols[dc]}
 
     npeers = (nf - 1) + max(pair, 1) * (nplace - 1)
     if npeers:
         barrier = pltpu.get_barrier_semaphore()
 
-        def greet_frame(k):
-            pl.semaphore_signal(
-                barrier, inc=1, device_id={"frame": lax.rem(me + k, nf)}, device_id_type=MESH
-            )
-
-        def greet_place(k):
-            where = lax.rem(place + 1 + k // max(pair, 1), nplace)
-            frame = lax.rem(k, max(pair, 1)) * 2 + lax.rem(me, 2)
-            pl.semaphore_signal(barrier, inc=1, device_id=there(frame, where), device_id_type=MESH)
-
-        loop(1, nf, greet_frame)
-        loop(0, max(pair, 1) * (nplace - 1), greet_place)
+        for k in range(1, nf):
+            pl.semaphore_signal(barrier, inc=1, device_id={"frame": frames[k]}, device_id_type=MESH)
+        for x in others:
+            if x[1:] != (0, 0):
+                pl.semaphore_signal(barrier, inc=1, device_id=there(x), device_id_type=MESH)
 
     coefs[...] = jnp.zeros((ITEMS, 128), F32)
     bent[...] = jnp.zeros((ITEMS * 16, 128), F32)
@@ -430,60 +436,50 @@
     def owner(s, k):
         return lax.rem(s, 2) * owners + k
 
-    def rs_copy(it, s, k, slot):
-        return remote(
-            sums.at[it, s, pl.ds(k * own, own)], parts.at[it, s // 2, slot],
-            rs_send.at[it, s, k], rs_recv.at[it, s // 2, slot], {"frame": owner(s, k)},
-        )
+    def landed(ref, sem):
+        pltpu.make_async_copy(ref, ref, sem).wait()
+
+    def mine(s):
+        return me // owners == lax.rem(s, 2) if nf > 1 else s >= 0
 
     def send_field(it, s):
         if nf > 1:
-            def act(k):
-                pl.when(owner(s, k) != me)(lambda: rs_copy(it, s, k, me).start())
-
-            loop(0, owners, act)
-
-    def rs_arrival(it, s, peer):
-        return remote(
-            sums.at[it, s, pl.ds(0, own)], parts.at[it, s // 2, peer],
-            rs_send.at[it, s, 0], rs_recv.at[it, s // 2, peer], {"frame": peer},
-        )
-
-    def ag_copy(it, s, k, peer):
-        at = pl.ds(k * own, own)
-        return remote(
-            objs.at[it, s, at], objs.at[it, s, at],
-            ag_send.at[it, s // 2, peer], ag_recv.at[it, s, k], {"frame": peer},
-        )
-
-    def mine(s):
-        return me // owners == lax.rem(s, 2) if nf > 1 else s >= 0
+            for k in range(owners):
+                peer = owner(s, k)
+                copy = remote(
+                    sums.at[it, s, pl.ds(k * own, own)], parts.at[it, s // 2, me],
+                    rs_send.at[it, s], rs_recv.at[it, s // 2], {"frame": peer},
+                )
+                pl.when(peer != me)(copy.start)
 
     def reduce_field(it, s):
         @pl.when(mine(s))
         def _():
             k = lax.rem(me, owners)
-            loop(1, nf, lambda j: rs_arrival(it, s, lax.rem(me + j, nf)).wait_recv())
+            if nf > 1:
+                landed(parts.at[it, s // 2, pl.ds(0, nf - 1)], rs_recv.at[it, s // 2])
             for j in range(own):
                 tile = k * own + j
                 total = sums[it, s, tile]
                 for other in range(1, nf):
-                    total = total + parts[it, s // 2, lax.rem(me + other, nf), j]
+                    total = total + parts[it, s // 2, frames[other], j]
                 first = tile == 0
                 real, imag, power = total[0], total[1], total[2]
                 n = noise[0, 0]
                 other = jnp.where(m00 & first, pltpu.roll(imag, 64, 1), power)
                 objs[it, s, tile, 0] = real / (power + n)
                 objs[it, s, tile, 1] = jnp.where(m064 & first, 0.0, imag / (other + n))
-            loop(1, nf, lambda j: ag_copy(it, s, k, lax.rem(me + j, nf)).start())
+            at = pl.ds(k * own, own)
+            for j in range(1, nf):
+                remote(
+                    objs.at[it, s, at], objs.at[it, s, at],
+                    ag_send.at[it, s // 2], ag_recv.at[it, s], {"frame": frames[j]},
+                ).start()
 
     def wait_field(it, s):
         if nf > 1:
-            def act(k):
-                peer = owner(s, k)
-                pl.when(peer != me)(lambda: ag_copy(it, s, k, peer).wait_recv())
-
-            loop(0, owners, act)
+            pl.when(mine(s))(lambda: landed(objs.at[it, s, pl.ds(0, TILES - own)], ag_recv.at[it, s]))
+            pl.when(jnp.logical_not(mine(s)))(lambda: landed(objs.at[it, s], ag_recv.at[it, s]))
 
     def n1_copy(it, slot):
         return remote(
@@ -491,12 +487,10 @@
             n1_send.at[it], n1_recv.at[it], {"frame": me + 1 - 2 * lax.rem(me, 2)},
         )
 
-    def n2_copy(it, k):
-        frame, where = chip_at(k)
+    def n2_copy(it, steps):
         slot = me // 2 * nplace + place
         return remote(
-            norm2.at[it, slot], norm2.at[it, slot],
-            n2_send.at[it], n2_recv.at[it], there(frame, where),
+            norm2.at[it, slot], norm2.at[it, slot], n2_send.at[it], n2_recv.at[it], there(steps)
         )
 
     def halo_copies(it):
@@ -722,10 +716,8 @@
             if npeers:
                 pl.when((it == 0) & (s == 0))(lambda: pl.semaphore_wait(barrier, npeers))
             send_field(it, s)
-            pl.when(s >= 2)(lambda: reduce_field(it, s - 2))
 
         def backward_step(s):
-            pl.when(s < 2)(lambda: reduce_field(it, s + 2))
             wait_field(it, s)
             backward(it, s)
 
@@ -735,6 +727,7 @@
         for inside, copy in halo_copies(it):
             pl.when(inside)(copy.start)
 
+        loop(0, FIELDS, lambda s: reduce_field(it, s))
         loop(0, FIELDS, backward_step)
 
         x = jnp.concatenate([dbent[pl.ds(i, ITEMS, stride=16), :] for i in range(TERMS)], axis=1)
@@ -752,12 +745,13 @@
             n1_copy(it, 1 - lax.rem(me, 2)).wait_recv()
             total = norm1[it, 0] + norm1[it, 1]
         norm2[it, slot] = total
-        loop(1, chips, lambda k: n2_copy(it, k).start())
+        for x in others:
+            n2_copy(it, x).start()
 
         for side, inside in halo_sides():
             @pl.when(inside)
             def _(side=side):
-                pltpu.make_async_copy(halo.at[it, side], halo.at[it, side], h_recv.at[it, side]).wait()
+                landed(halo.at[it, side], h_recv.at[it, side])
 
         above, below = halo[it, 0, 8:], halo[it, 1, :8]
         laplace = []
@@ -774,8 +768,7 @@
         laplace = jnp.concatenate(laplace, axis=0)
 
         if chips > 1:
-            rest = pl.ds(0, chips - 1)
-            pltpu.make_async_copy(norm2.at[it, rest], norm2.at[it, rest], n2_recv.at[it]).wait()
+            landed(norm2.at[it, pl.ds(0, chips - 1)], n2_recv.at[it])
         total = jnp.sum(jnp.sum(norm2[it], axis=0), axis=1, keepdims=True)
         count = ITEMS * MODES * nf * nplace
         scale = jnp.sqrt(total / count + TINY)
@@ -784,21 +777,18 @@
     def departures(it):
         if nf > 1:
             def field(s):
-                def act(k):
-                    pl.when(owner(s, k) != me)(lambda: rs_copy(it, s, k, me).wait_send())
-
-                loop(0, owners, act)
-
                 @pl.when(mine(s))
                 def _():
-                    k = lax.rem(me, owners)
-                    loop(1, nf, lambda j: ag_copy(it, s, k, lax.rem(me + j, nf)).wait_send())
+                    if own < TILES:
+                        landed(sums.at[it, s, pl.ds(0, TILES - own)], rs_send.at[it, s])
+                    landed(parts.at[it, s // 2, pl.ds(0, nf - 1), :, pl.ds(0, 2)], ag_send.at[it, s // 2])
+
+                pl.when(jnp.logical_not(mine(s)))(lambda: landed(sums.at[it, s], rs_send.at[it, s]))
 
             loop(0, FIELDS, field)
             n1_copy(it, lax.rem(me, 2)).wait_send()
         if chips > 1:
-            rest = pl.ds(0, chips - 1)
-            pltpu.make_async_copy(norm2.at[it, rest], norm2.at[it, rest], n2_send.at[it]).wait()
+            landed(norm2.at[it, pl.ds(0, chips - 1)], n2_send.at[it])
         for inside, copy in halo_copies(it):
             pl.when(inside)(copy.wait_send)
 
@@ -873,8 +863,7 @@
             pltpu.VMEM((HALF, 128), F32),
         ]
         dma = pltpu.SemaphoreType.DMA
-        scratch += [dma((ITERS, FIELDS, TILES)), dma((ITERS, 2, nf))]
-        scratch += [dma((ITERS, 2, nf)), dma((ITERS, FIELDS, TILES))]
+        scratch += [dma((ITERS, FIELDS)), dma((ITERS, 2)), dma((ITERS, 2)), dma((ITERS, FIELDS))]
         scratch += [dma((ITERS,)) for _ in range(4)]
         scratch += [dma((ITERS, 4)) for _ in range(2)]
         single = lambda x: x.reshape(1, 1)

time: 74.7 us -> 68.7 us (0.920)
  Pallas kernels: 69.2 us -> 63.2 us
    pallas_call x1, Pallas kernels: 69.2 us -> 63.2 us  [body(): pl.pallas_call(functools.partial(kernel, nf, nr, nc), out_shape=(jax.Shap...]
where the time goes in v4:
time: 68.7 us; the launch traced here: 68.5 us
  Pallas kernels  63.2 us (92%)
  local copies, waits for them, and re-layouts  2.67 us (4%)
  between operations  2.58 us (4%)
    pallas_call x1, Pallas kernels, body(): pl.pallas_call(functools.partial(kernel, nf, nr, nc), out_shape=(jax.Shap...  63.2 us
    unnamed x2, local copies, waits for them, and re-layouts  2.67 us

profile of v4, /device:TPU:1, one launch (start us, length us, event | category | flops | bytes accessed | tf_op | source)
XLA Modules:
  0.0 68.5 jit_solution(9685387724886862506)
XLA Ops:
  2.6 63.2 %shard_map.239 = (f32[4,2,2,36]{3,2,1,0:T(2,128)}, f32[2,2,2,8,128]{4,3,2,1,0:T(8,128)}) custom-call(bf16[4,2,2,2,128,128]{5,4,3,2,1,0:T(8,128)(2,1)} %images.1, s32[2,2,2,4]{3,2,1,0:T(2,128)} %bitcast.7, s32[2,2]{1,0:T(2,128)} %kinds.1, f32[4,2,2,36]{3,2,1,0:T(2,128)} %coefs_in.1, f32[1,1]{1,0:T(1,128)} %bitcast.4.step, f32[1,1]{1,0:T(1,128)} %bitcast.5.noise, ...), custom_call_target="tpu_custom_call" | custom-call | tf_op jit(solution)/shard_map/pallas_call | solution.py:870
  65.8 1.3 %copy.31 = f32[4,2,2,36]{3,2,1,0:T(2,128)} copy(f32[4,2,2,36]{3,2,1,0:T(2,128)} %get-tuple-element.4) | data formatting | bytes 4608
  67.1 1.4 %copy.32 = f32[2,2,2,8,128]{4,3,2,1,0:T(8,128)} copy(f32[2,2,2,8,128]{4,3,2,1,0:T(8,128)} %get-tuple-element.5) | data formatting | bytes 65536

commit v5 on v4

--- a/solution.py
+++ b/solution.py
@@ -13,6 +13,10 @@
 ITERS = 2
 MODES = 36
 SKEW = 3
+ORDER = (
+    ("r", 0), ("w", 0), ("r", 1), ("w", 1), ("q", 0), ("q", 1), ("q", 2), ("q", 3),
+    ("l", 0), ("l", 1), ("v", 0), ("l", 2), ("l", 3), ("v", 1),
+)
 GROUP = 2
 DEGREE = 9
 TERMS = DEGREE + 1
@@ -201,9 +205,9 @@
         w1t=w1t,
         turn65=turn65,
         l2=left_table(l2),
-        l2t=left_table(l2.T),
+        l2t=tall_table(l2.T),
         q=left_table(q),
-        qt=left_table(qt),
+        qt=tall_table(qt),
         w4=right_table(w4),
         w4t=right_table(w4.T),
         qd=qd.astype(np.float32),
@@ -220,6 +224,9 @@
 NAMES = (
     "w1", "w1t", "turn65", "l2", "l2t", "q", "qt", "w4", "w4t", "qd", "t1", "t2", "y1", "y2", "lens", "taper", "flip",
 )
+
+
+MOVED = ("w1", "w1t", "l2", "l2t", "q", "qt", "w4", "w4t", "t1", "t2", "flip")
 
 
 def sincos(x):
@@ -296,6 +303,17 @@
         second(x)
 
 
+def tall_table(matrix):
+    hi, lo = pieces(matrix, 2)
+    return np.concatenate([np.concatenate([hi, hi], 1), np.concatenate([lo, 0 * lo], 1)], 0)
+
+
+def tall(table, x):
+    out = jnp.dot(table, jnp.concatenate(two(x), axis=0), preferred_element_type=F32)
+    half = out.shape[0] // 2
+    return out[:half] + out[half:]
+
+
 def patched(whole, first):
     return jnp.concatenate([first, whole[8:]], axis=0)
 
@@ -305,6 +323,8 @@
     images, corners, kinds, coefs_in, step, noise, smooth,
     w1, w1t, turn65, l2, l2t, q, qt, w4, w4t, qd, t1, t2, y1, y2, lens, taper, flip,
     coefs_out, object_out,
+    images_, w1_, w1t_, l2_, l2t_, q_, qt_, w4_, w4t_, t1_, t2_, flip_, result,
+    fill_sem, image_sem, result_sem,
     coefs, halo, bent, dbent, fields, waves, otf, data, sums, parts, objs, norm1, norm2, turned,
     rs_send, rs_recv, ag_send, ag_recv, n1_send, n1_recv, n2_send, n2_recv, h_send, h_recv,
 ):
@@ -359,11 +379,39 @@
     if npeers:
         barrier = pltpu.get_barrier_semaphore()
 
-        for k in range(1, nf):
-            pl.semaphore_signal(barrier, inc=1, device_id={"frame": frames[k]}, device_id_type=MESH)
         for x in others:
             if x[1:] != (0, 0):
                 pl.semaphore_signal(barrier, inc=1, device_id=there(x), device_id_type=MESH)
+        for k in range(1, nf):
+            pl.semaphore_signal(barrier, inc=1, device_id={"frame": frames[k]}, device_id_type=MESH)
+
+    fills = {
+        i: pltpu.make_async_copy(src, dst, fill_sem.at[i])
+        for i, (src, dst) in enumerate(
+            [
+                (w4, w4_), (t1, t1_), (w1, w1_), (l2, l2_), (q, q_), (w4t, w4t_), (qt, qt_),
+                (l2t, l2t_), (w1t, w1t_), (t2, t2_), (flip, flip_),
+            ]
+        )
+    }
+    source = images
+
+    def image_copy(s, f):
+        r, c_ = s // 2, lax.rem(s, 2)
+        return pltpu.make_async_copy(source.at[f, r, c_], images_.at[s, f], image_sem.at[s, f])
+
+    for f in range(FRAMES):
+        image_copy(0, f).start()
+    for i in range(5):
+        fills[i].start()
+    for s in range(1, FIELDS):
+        for f in range(FRAMES):
+            image_copy(s, f).start()
+    for i in range(5, len(fills)):
+        fills[i].start()
+    images, w1, w1t, l2, l2t, q, qt, w4, w4t, t1, t2, flip = (
+        images_, w1_, w1t_, l2_, l2t_, q_, qt_, w4_, w4t_, t1_, t2_, flip_
+    )
 
     coefs[...] = jnp.zeros((ITEMS, 128), F32)
     bent[...] = jnp.zeros((ITEMS * 16, 128), F32)
@@ -376,6 +424,8 @@
 
     def data_field(s):
         r, c_ = s // 2, lax.rem(s, 2)
+        for f in range(FRAMES):
+            image_copy(s, f).wait()
         kind = kinds[r, c_]
         window = jnp.where(
             kind == 0, taper[pl.ds(0, 1), :],
@@ -392,7 +442,7 @@
         for f in range(FRAMES):
             c0 = corners[0, r, c_, f].astype(F32)
             c1 = corners[1, r, c_, f].astype(F32)
-            image = jnp.concatenate([images[f, r, c_, 0], images[f, r, c_, 1]], axis=1)
+            image = jnp.concatenate([images[s, f, 0], images[s, f, 1]], axis=1)
             lines = jnp.dot(
                 rotor, jnp.concatenate([image, image], axis=0), preferred_element_type=F32
             )
@@ -425,8 +475,6 @@
                     di, jnp.where(m00, middle[f * 2 + c], di[:8])
                 )
 
-    loop(0, FIELDS, data_field)
-
     def remote(src, dst, send, recv, device):
         return pltpu.make_async_remote_copy(
             src_ref=src, dst_ref=dst, send_sem=send, recv_sem=recv,
@@ -444,7 +492,8 @@
 
     def send_field(it, s):
         if nf > 1:
-            for k in range(owners):
+            for step_ in range(owners):
+                k = lax.rem(me + step_, owners)
                 peer = owner(s, k)
                 copy = remote(
                     sums.at[it, s, pl.ds(k * own, own)], parts.at[it, s // 2, me],
@@ -470,7 +519,7 @@
                 objs[it, s, tile, 0] = real / (power + n)
                 objs[it, s, tile, 1] = jnp.where(m064 & first, 0.0, imag / (other + n))
             at = pl.ds(k * own, own)
-            for j in range(1, nf):
+            for j in sorted(range(1, nf), key=lambda j: -min(j // 4, 4 - j // 4) - j // 2 % 2):
                 remote(
                     objs.at[it, s, at], objs.at[it, s, at],
                     ag_send.at[it, s // 2], ag_recv.at[it, s], {"frame": frames[j]},
@@ -515,6 +564,25 @@
         if nc > 1:
             out += [(2, col > 0), (3, col < nc - 1)]
         return out
+
+    def bend(cf):
+        ch = cf.astype(BF16).astype(F32)
+        cm = (cf - ch).astype(BF16).astype(F32)
+        cl = (cf - ch - cm).astype(BF16).astype(F32)
+        low = ch + pltpu.roll(cm, 36, 1) + pltpu.roll(ch, 72, 1)
+        high = cl + pltpu.roll(ch, 36, 1) + pltpu.roll(cm, 72, 1)
+        lhs = jnp.concatenate([low, high], axis=1).astype(BF16)
+        return jnp.dot(lhs, t1[...], preferred_element_type=F32)
+
+    def store_bent(out):
+        for i in range(TERMS):
+            bent[pl.ds(i, ITEMS, stride=16), :] = out[:, i * 128 : i * 128 + 128]
+
+    fills[0].wait()
+    fills[1].wait()
+    store_bent(bend(coefs[...]))
+    for i in range(2, 5):
+        fills[i].wait()
 
     def forward(it, s):
         stacks = []
@@ -609,8 +677,10 @@
             sums[it, s, t, 2] = pw
 
     def backward(it, s):
-        dz = []
-        for g in range(0, FRAMES, GROUP):
+        dz = {}
+        zero = subs == 0
+
+        def residual(g):
             res = [[] for _ in range(2 * GROUP)]
             for t in range(TILES):
                 our = objs[it, s, t, 0]
@@ -632,21 +702,19 @@
                             ii = jnp.where(m00, 0.0, ii)
                         real = dr * our + ii - oor * zr
                         res[(f - g) * 2 + c].append(jnp.concatenate([real, im - ooi * zi], axis=1))
-            dz.append(right(jnp.concatenate(sum(res, []), axis=0), w4t[...]))
-        dz = jnp.concatenate(dz, axis=0)
-        dlines = []
-        zero = subs == 0
+            return jnp.concatenate(sum(res, []), axis=0)
 
         def first(f):
-            at = f * 128
+            at = f % GROUP * 128
+            dz_ = dz[f // GROUP]
             half = jnp.concatenate(
                 [
-                    jnp.concatenate([dz[at : at + 64, :128], dz[at + 64 : at + 128, :128]], axis=1),
-                    jnp.concatenate([dz[at : at + 64, 128:], dz[at + 64 : at + 128, 128:]], axis=1),
+                    jnp.concatenate([dz_[at : at + 64, :128], dz_[at + 64 : at + 128, :128]], axis=1),
+                    jnp.concatenate([dz_[at : at + 64, 128:], dz_[at + 64 : at + 128, 128:]], axis=1),
                 ],
                 axis=0,
             )
-            dspread = left(qt[...], half)
+            dspread = tall(qt[...], half)
             dwaves = []
             for c in range(2):
                 de = dspread[:64, c * 128 : c * 128 + 128]
@@ -669,23 +737,32 @@
             return dwaves
 
         def second(dwaves):
+            out = []
             for dwave in dwaves:
-                x = left(l2t[...], dwave)
-                dlines.append(
-                    jnp.concatenate([x[:64], x[64:72] * turn65[...], x[72:]], axis=0)
-                )
-
-        def third():
-            if len(dlines) % (2 * GROUP) == 0:
-                x = jnp.concatenate(dlines[-2 * GROUP :], axis=0)
-                x = jnp.dot(
-                    jnp.concatenate(two(x), axis=1), w1t[...], preferred_element_type=F32
-                )
-                dpupil.append(x[:, :128] + x[:, 128:])
-
-        dpupil = []
-        skewed(FRAMES, SKEW, first, lambda x: (second(x), third()))
-        dpupil = jnp.concatenate(dpupil, axis=0)
+                x = tall(l2t[...], dwave)
+                out.append(jnp.concatenate([x[:64], x[64:72] * turn65[...], x[72:]], axis=0))
+            return out
+
+        def third(x):
+            x = jnp.dot(
+                jnp.concatenate(two(jnp.concatenate(x, axis=0)), axis=1), w1t[...],
+                preferred_element_type=F32,
+            )
+            return x[:, :128] + x[:, 128:]
+
+        res, dwaves, dlines, dpupil = {}, {}, {}, {}
+        for what, i in ORDER:
+            if what == "r":
+                res[i] = residual(i * GROUP)
+            elif what == "w":
+                dz[i] = right(res[i], w4t[...])
+            elif what == "q":
+                dwaves[i] = first(i)
+            elif what == "l":
+                dlines[i] = second(dwaves[i])
+            else:
+                dpupil[i] = third(sum([dlines[f] for f in range(i * GROUP, i * GROUP + GROUP)], []))
+        dpupil = jnp.concatenate([dpupil[i] for i in sorted(dpupil)], axis=0)
         dphase = []
         for f in range(FRAMES):
             at = f * 2 * PAD
@@ -699,23 +776,58 @@
         for f in range(FRAMES):
             dbent[pl.ds(pl.multiple_of((s * 4 + f) * 16, 16), 16), :] = out[:, f * 128 : f * 128 + 128]
 
+    def result_copy():
+        return pltpu.make_async_copy(result, object_out, result_sem)
+
+    def write_object():
+        last = ITERS - 1
+        for j in range(per):
+            tile = me * per + j
+
+            @pl.when(tile < 8)
+            def _(j=j, tile=tile):
+                for s in range(FIELDS):
+                    re = objs[last, s, tile, 0]
+                    im = objs[last, s, tile, 1]
+                    result[0, s // 2, s % 2, pl.ds(j * 8, 8), :] = re
+                    result[1, s // 2, s % 2, pl.ds(j * 8, 8), :] = jnp.where(m00 & (tile == 0), 0.0, im)
+
+            @pl.when(tile >= 8)
+            def _(j=j, tile=tile):
+                g = tile - 8
+                for s in range(FIELDS):
+                    for c in range(2):
+                        at = (s * 2 + c) * 8
+                        for i in range(1, 8):
+                            turned[pl.ds(at + i, 1), :] = objs[last, s, 7 - g, c, pl.ds(8 - i, 1), :]
+                        zero = objs[last, s, lax.rem(8 - g, 8), c, pl.ds(0, 1), :]
+                        if c == 0:
+                            middle = objs[last, s, 0, 1, pl.ds(0, 1), :]
+                            middle = jnp.where(lanes[:1] == 0, middle, 0.0)
+                        else:
+                            middle = jnp.zeros((1, 128), F32)
+                        turned[pl.ds(at, 1), :] = jnp.where(g == 0, middle, zero)
+                out = jnp.dot(
+                    jnp.concatenate(three(turned[...]), axis=1), flip[...], preferred_element_type=F32
+                )
+                for s in range(FIELDS):
+                    at = s * 16
+                    result[0, s // 2, s % 2, pl.ds(j * 8, 8), :] = out[at : at + 8]
+                    result[1, s // 2, s % 2, pl.ds(j * 8, 8), :] = -out[at + 8 : at + 16]
+        result_copy().start()
+
     def iteration(it):
         cf = coefs[...]
-        ch = cf.astype(BF16).astype(F32)
-        cm = (cf - ch).astype(BF16).astype(F32)
-        cl = (cf - ch - cm).astype(BF16).astype(F32)
-        low = ch + pltpu.roll(cm, 36, 1) + pltpu.roll(ch, 72, 1)
-        high = cl + pltpu.roll(ch, 36, 1) + pltpu.roll(cm, 72, 1)
-        lhs = jnp.concatenate([low, high], axis=1).astype(BF16)
-        out = jnp.dot(lhs, t1[...], preferred_element_type=F32)
-        for i in range(TERMS):
-            bent[pl.ds(i, ITEMS, stride=16), :] = out[:, i * 128 : i * 128 + 128]
 
         def forward_step(s):
+            pl.when(it == 0)(lambda: data_field(s))
             forward(it, s)
+
+            first = (it == 0) & (s == 2)
             if npeers:
-                pl.when((it == 0) & (s == 0))(lambda: pl.semaphore_wait(barrier, npeers))
-            send_field(it, s)
+                pl.when(first)(lambda: pl.semaphore_wait(barrier, npeers))
+            pl.when(first)(lambda: loop(0, 2, lambda s: send_field(it, s)))
+            pl.when((it > 0) | (s >= 2))(lambda: send_field(it, s))
 
         def backward_step(s):
             wait_field(it, s)
@@ -728,6 +840,12 @@
             pl.when(inside)(copy.start)
 
         loop(0, FIELDS, lambda s: reduce_field(it, s))
+
+        @pl.when(it == 0)
+        def _():
+            for i in range(5, len(fills)):
+                fills[i].wait()
+
         loop(0, FIELDS, backward_step)
 
         x = jnp.concatenate([dbent[pl.ds(i, ITEMS, stride=16), :] for i in range(TERMS)], axis=1)
@@ -766,13 +884,18 @@
             out = 4.0 * mine_ - other - pltpu.roll(mine_, 4, 0) - beside
             laplace.append(out - (above if r == 0 else below))
         laplace = jnp.concatenate(laplace, axis=0)
+        smoothed = cf - step[0, 0] * smooth[0, 0] * laplace
+        out = bend(jnp.concatenate([smoothed, grads], axis=0))
+        pl.when(it == ITERS - 1)(write_object)
 
         if chips > 1:
             landed(norm2.at[it, pl.ds(0, chips - 1)], n2_recv.at[it])
         total = jnp.sum(jnp.sum(norm2[it], axis=0), axis=1, keepdims=True)
         count = ITEMS * MODES * nf * nplace
         scale = jnp.sqrt(total / count + TINY)
-        coefs[...] = cf - step[0, 0] * (grads / scale + smooth[0, 0] * laplace)
+        pace = step[0, 0] / scale
+        coefs[...] = smoothed - pace * grads
+        store_bent(out[:ITEMS] - pace * out[ITEMS:])
 
     def departures(it):
         if nf > 1:
@@ -798,41 +921,7 @@
         for s in range(FIELDS):
             coefs_out[f, s // 2, pl.ds(s % 2, 1), :] = coefs[pl.ds(s * 4 + f, 1), pl.ds(0, MODES)]
 
-    last = ITERS - 1
-    for j in range(per):
-        tile = me * per + j
-
-        @pl.when(tile < 8)
-        def _(j=j, tile=tile):
-            for s in range(FIELDS):
-                re = objs[last, s, tile, 0]
-                im = objs[last, s, tile, 1]
-                object_out[0, s // 2, s % 2, pl.ds(j * 8, 8), :] = re
-                object_out[1, s // 2, s % 2, pl.ds(j * 8, 8), :] = jnp.where(m00 & (tile == 0), 0.0, im)
-
-        @pl.when(tile >= 8)
-        def _(j=j, tile=tile):
-            g = tile - 8
-            for s in range(FIELDS):
-                for c in range(2):
-                    at = (s * 2 + c) * 8
-                    for i in range(1, 8):
-                        turned[pl.ds(at + i, 1), :] = objs[last, s, 7 - g, c, pl.ds(8 - i, 1), :]
-                    zero = objs[last, s, lax.rem(8 - g, 8), c, pl.ds(0, 1), :]
-                    if c == 0:
-                        middle = objs[last, s, 0, 1, pl.ds(0, 1), :]
-                        middle = jnp.where(lanes[:1] == 0, middle, 0.0)
-                    else:
-                        middle = jnp.zeros((1, 128), F32)
-                    turned[pl.ds(at, 1), :] = jnp.where(g == 0, middle, zero)
-            out = jnp.dot(
-                jnp.concatenate(three(turned[...]), axis=1), flip[...], preferred_element_type=F32
-            )
-            for s in range(FIELDS):
-                at = s * 16
-                object_out[0, s // 2, s % 2, pl.ds(j * 8, 8), :] = out[at : at + 8]
-                object_out[1, s // 2, s % 2, pl.ds(j * 8, 8), :] = -out[at + 8 : at + 16]
-
+    result_copy().wait()
     loop(0, ITERS, departures)
 
 
@@ -842,11 +931,20 @@
     per = 16 // nf
     vmem = pl.BlockSpec(memory_space=pltpu.VMEM)
     smem = pl.BlockSpec(memory_space=pltpu.SMEM)
+    hbm = pl.BlockSpec(memory_space=pl.ANY)
 
     def body(images, corners, kinds, coefs, step, noise, smooth):
         own = min(per, TILES)
         chips = max(nf // 2, 1) * nr * nc
-        scratch = [
+        scratch = [pltpu.VMEM((FIELDS, FRAMES, 2, PIXELS, PIXELS), BF16)]
+        scratch += [pltpu.VMEM(host[name].shape, BF16) for name in MOVED]
+        scratch += [
+            pltpu.VMEM((2, 2, 2, 8 * per, 128), F32),
+            pltpu.SemaphoreType.DMA((len(MOVED),)),
+            pltpu.SemaphoreType.DMA((FIELDS, FRAMES)),
+            pltpu.SemaphoreType.DMA,
+        ]
+        scratch += [
             pltpu.VMEM((ITEMS, 128), F32),
             pltpu.VMEM((ITERS, 5, ITEMS, 128), F32),
             pltpu.VMEM((ITEMS * 16, 128), F32),
@@ -873,8 +971,9 @@
                 jax.ShapeDtypeStruct((FRAMES, 2, 2, MODES), F32),
                 jax.ShapeDtypeStruct((2, 2, 2, 8 * per, 128), F32),
             ),
-            in_specs=[vmem, smem, smem, vmem, smem, smem, smem] + [vmem] * len(NAMES),
-            out_specs=(vmem, vmem),
+            in_specs=[hbm, smem, smem, vmem, smem, smem, smem]
+            + [hbm if name in MOVED else vmem for name in NAMES],
+            out_specs=(vmem, hbm),
             scratch_shapes=scratch,
             compiler_params=pltpu.CompilerParams(
                 collective_id=0 if nf * nr * nc > 1 else None,

time: 68.7 us -> 67.4 us (0.981)
  Pallas kernels: 63.2 us -> 61.9 us
    pallas_call x1, Pallas kernels: 63.2 us -> 61.9 us  [body(): pl.pallas_call(functools.partial(kernel, nf, nr, nc), out_shape=(jax.Shap...]
where the time goes in v5:
time: 67.4 us; the launch traced here: 67.1 us
  Pallas kernels  61.9 us (92%)
  local copies, waits for them, and re-layouts  2.67 us (4%)
  between operations  2.58 us (4%)
    pallas_call x1, Pallas kernels, body(): pl.pallas_call(functools.partial(kernel, nf, nr, nc), out_shape=(jax.Shap...  61.9 us
    unnamed x2, local copies, waits for them, and re-layouts  2.67 us

profile of v5, /device:TPU:1, one launch (start us, length us, event | category | flops | bytes accessed | tf_op | source)
XLA Modules:
  0.0 67.1 jit_solution(2789447718344716560)
XLA Ops:
  2.6 61.9 %shard_map.239 = (f32[4,2,2,36]{3,2,1,0:T(2,128)}, f32[2,2,2,8,128]{4,3,2,1,0:T(8,128)}) custom-call(bf16[4,2,2,2,128,128]{5,4,3,2,1,0:T(8,128)(2,1)} %images.1, s32[2,2,2,4]{3,2,1,0:T(2,128)} %bitcast.7, s32[2,2]{1,0:T(2,128)} %kinds.1, f32[4,2,2,36]{3,2,1,0:T(2,128)} %coefs_in.1, f32[1,1]{1,0:T(1,128)} %bitcast.4.step, f32[1,1]{1,0:T(1,128)} %bitcast.5.noise, ...), custom_call_target="tpu_custom_call" | custom-call | tf_op jit(solution)/shard_map/pallas_call | solution.py:968
  64.4 1.3 %copy.31 = f32[4,2,2,36]{3,2,1,0:T(2,128)} copy(f32[4,2,2,36]{3,2,1,0:T(2,128)} %get-tuple-element.4) | data formatting | bytes 4608
  65.7 1.4 %copy.32 = f32[2,2,2,8,128]{4,3,2,1,0:T(8,128)} copy(f32[2,2,2,8,128]{4,3,2,1,0:T(8,128)} %get-tuple-element.5) | data formatting | bytes 65536

commit v6 on v5

--- a/solution.py
+++ b/solution.py
@@ -354,37 +354,6 @@
 
     halo[...] = jnp.zeros(halo.shape, F32)
 
-    def after(index, step, count):
-        moved = index + step
-        return jnp.where(moved >= count, moved - count, moved)
-
-    frames = [after(me, k, nf) for k in range(nf)]
-    rows = [after(row, k, nr) for k in range(nr)]
-    cols = [after(col, k, nc) for k in range(nc)]
-
-    def far(steps):
-        k, dr, dc = steps
-        dy, dx = k // 2, dc * 2 + k % 2
-        return min(dy, 4 - dy) + min(dr, nr - dr) + min(dx, 4 - dx)
-
-    others = [(k, dr, dc) for k in range(max(pair, 1)) for dr in range(nr) for dc in range(nc)]
-    others = sorted(others, key=far, reverse=True)
-    others = [x for x in others if x != (0, 0, 0)]
-
-    def there(steps):
-        k, dr, dc = steps
-        return {"frame": frames[2 * k], "row": rows[dr], "col": cols[dc]}
-
-    npeers = (nf - 1) + max(pair, 1) * (nplace - 1)
-    if npeers:
-        barrier = pltpu.get_barrier_semaphore()
-
-        for x in others:
-            if x[1:] != (0, 0):
-                pl.semaphore_signal(barrier, inc=1, device_id=there(x), device_id_type=MESH)
-        for k in range(1, nf):
-            pl.semaphore_signal(barrier, inc=1, device_id={"frame": frames[k]}, device_id_type=MESH)
-
     fills = {
         i: pltpu.make_async_copy(src, dst, fill_sem.at[i])
         for i, (src, dst) in enumerate(
@@ -412,6 +381,37 @@
     images, w1, w1t, l2, l2t, q, qt, w4, w4t, t1, t2, flip = (
         images_, w1_, w1t_, l2_, l2t_, q_, qt_, w4_, w4t_, t1_, t2_, flip_
     )
+
+    def after(index, step, count):
+        moved = index + step
+        return jnp.where(moved >= count, moved - count, moved)
+
+    frames = [after(me, k, nf) for k in range(nf)]
+    rows = [after(row, k, nr) for k in range(nr)]
+    cols = [after(col, k, nc) for k in range(nc)]
+
+    def far(steps):
+        k, dr, dc = steps
+        dy, dx = k // 2, dc * 2 + k % 2
+        return min(dy, 4 - dy) + min(dr, nr - dr) + min(dx, 4 - dx)
+
+    others = [(k, dr, dc) for k in range(max(pair, 1)) for dr in range(nr) for dc in range(nc)]
+    others = sorted(others, key=far, reverse=True)
+    others = [x for x in others if x != (0, 0, 0)]
+
+    def there(steps):
+        k, dr, dc = steps
+        return {"frame": frames[2 * k], "row": rows[dr], "col": cols[dc]}
+
+    npeers = (nf - 1) + max(pair, 1) * (nplace - 1)
+    if npeers:
+        barrier = pltpu.get_barrier_semaphore()
+
+        for x in others:
+            if x[1:] != (0, 0):
+                pl.semaphore_signal(barrier, inc=1, device_id=there(x), device_id_type=MESH)
+        for k in range(1, nf):
+            pl.semaphore_signal(barrier, inc=1, device_id={"frame": frames[k]}, device_id_type=MESH)
 
     coefs[...] = jnp.zeros((ITEMS, 128), F32)
     bent[...] = jnp.zeros((ITEMS * 16, 128), F32)
@@ -925,6 +925,11 @@
     loop(0, ITERS, departures)
 
 
+def deliver(coefs, objects, coefs_out, object_out):
+    coefs_out[...] = coefs[...]
+    object_out[...] = objects[...]
+
+
 def solution(mesh):
     nf, nr, nc = (mesh.shape[name] for name in ("frame", "row", "col"))
     host = tables()
@@ -965,7 +970,7 @@
         scratch += [dma((ITERS,)) for _ in range(4)]
         scratch += [dma((ITERS, 4)) for _ in range(2)]
         single = lambda x: x.reshape(1, 1)
-        return pl.pallas_call(
+        raw = pl.pallas_call(
             functools.partial(kernel, nf, nr, nc),
             out_shape=(
                 jax.ShapeDtypeStruct((FRAMES, 2, 2, MODES), F32),
@@ -984,6 +989,12 @@
             images, corners.transpose(0, 2, 3, 1), kinds, coefs, single(step), single(noise), single(smooth),
             *[jnp.asarray(host[name]) for name in NAMES],
         )
+        return pl.pallas_call(
+            deliver,
+            out_shape=tuple(jax.ShapeDtypeStruct(x.shape, x.dtype) for x in raw),
+            in_specs=[vmem, vmem],
+            out_specs=(vmem, vmem),
+        )(*raw)
 
     in_specs = (
         P("frame", "row", "col", None, None, None),

time: 67.4 us -> 65.3 us (0.969)
  local copies, waits for them, and re-layouts: 2.67 us -> 0 us
    unnamed x2 -> x0, local copies, waits for them, and re-layouts: 2.67 us -> none
    pallas_call x0 -> x1, Pallas kernels: none -> 1.4 us  [body(): pl.pallas_call(deliver, out_shape=tuple((jax.ShapeDtypeStruct(x.shape, x....]
    pallas_call x1, Pallas kernels: 61.9 us -> 61.1 us  [body(): pl.pallas_call(functools.partial(kernel, nf, nr, nc), out_shape=(jax.Shap...]
where the time goes in v6:
time: 65.3 us; the launch traced here: 65.1 us
  Pallas kernels  62.5 us (96%)
  between operations  2.58 us (4%)
    pallas_call x1, Pallas kernels, body(): pl.pallas_call(functools.partial(kernel, nf, nr, nc), out_shape=(jax.Shap...  61.1 us
    pallas_call x1, Pallas kernels, body(): pl.pallas_call(deliver, out_shape=tuple((jax.ShapeDtypeStruct(x.shape, x....  1.4 us

profile of v6, /device:TPU:1, one launch (start us, length us, event | category | flops | bytes accessed | tf_op | source)
XLA Modules:
  0.0 65.1 jit_solution(3957556880326497339)
XLA Ops:
  2.6 61.1 %shard_map.239 = (f32[4,2,2,36]{3,2,1,0:T(2,128)}, f32[2,2,2,8,128]{4,3,2,1,0:T(8,128)}) custom-call(bf16[4,2,2,2,128,128]{5,4,3,2,1,0:T(8,128)(2,1)} %images.1, s32[2,2,2,4]{3,2,1,0:T(2,128)} %bitcast.7, s32[2,2]{1,0:T(2,128)} %kinds.1, f32[4,2,2,36]{3,2,1,0:T(2,128)} %coefs_in.1, f32[1,1]{1,0:T(1,128)} %bitcast.4.step, f32[1,1]{1,0:T(1,128)} %bitcast.5.noise, ...), custom_call_target="tpu_custom_call" | custom-call | tf_op jit(solution)/shard_map/pallas_call | solution.py:973
  63.7 1.4 %shard_map.240 = (f32[4,2,2,36]{3,2,1,0:T(2,128)}, f32[2,2,2,8,128]{4,3,2,1,0:T(8,128)}) custom-call(f32[4,2,2,36]{3,2,1,0:T(2,128)} %get-tuple-element.4.coefs, f32[2,2,2,8,128]{4,3,2,1,0:T(8,128)} %get-tuple-element.5.objects), custom_call_target="tpu_custom_call" | custom-call | tf_op jit(solution)/shard_map/pallas_call | solution.py:992

commit v7 on v6

--- a/solution.py
+++ b/solution.py
@@ -163,7 +163,7 @@
     t2[:, :MODES] = th.reshape(MODES, -1).T
     t2[:, 64 : 64 + MODES] = tm.reshape(MODES, -1).T
 
-    y = np.zeros((SIDE, 16))
+    y = np.zeros((PAD, 16))
     y[:65, :DEGREE] = rows_table
     y[65, DEGREE] = 1.0
     yh, ym, yl = pieces(y, 3)
@@ -436,25 +436,35 @@
         )
         rotor = jnp.concatenate(two(qd[...] * window), axis=1)
         both = jnp.concatenate([window, window], axis=1)
+        c0s = [corners[0, r, c_, f].astype(F32) for f in range(FRAMES)]
+        c1s = [corners[1, r, c_, f].astype(F32) for f in range(FRAMES)]
+
+        def choose(index, values):
+            out = jnp.where(index == 0, values[0], values[1])
+            return jnp.where(index == 2, values[2], jnp.where(index == 3, values[3], out))
+
+        cycles = rows64 * (choose(lanes[:1] // 32, c0s) * np.float32(1.0 / PIXELS))
+        cycles = cycles - jnp.floor(cycles + 0.5)
+        row_sin, row_cos = sincos(cycles * np.float32(2.0 * math.pi))
+        cycles = cols8 * (choose(subs, c1s) * np.float32(1.0 / PIXELS))
+        cycles = cycles - jnp.floor(cycles + 0.5)
+        col_sin, col_cos = sincos(cycles * np.float32(2.0 * math.pi))
+        col_sin = col_sin * np.float32(1.0 / PIXELS)
+        col_cos = col_cos * np.float32(1.0 / PIXELS)
+
         ready = []
         middle = []
         turns = []
         for f in range(FRAMES):
-            c0 = corners[0, r, c_, f].astype(F32)
-            c1 = corners[1, r, c_, f].astype(F32)
             image = jnp.concatenate([images[s, f, 0], images[s, f, 1]], axis=1)
             lines = jnp.dot(
                 rotor, jnp.concatenate([image, image], axis=0), preferred_element_type=F32
             )
             lines = lines * both
-            cycles = rows64 * (c0 * np.float32(1.0 / PIXELS))
-            cycles = cycles - jnp.floor(cycles + 0.5)
-            rs, rc = sincos(cycles * np.float32(2.0 * math.pi))
-            cycles = cols8 * (c1 * np.float32(1.0 / PIXELS))
-            cycles = cycles - jnp.floor(cycles + 0.5)
-            cs, cc = sincos(cycles * np.float32(2.0 * math.pi))
-            turns.append((cs[:1] * np.float32(1.0 / PIXELS), cc[:1] * np.float32(1.0 / PIXELS)))
-            c0h = c0 * 0.5
+            rs = jnp.broadcast_to(row_sin[:, f * 32 : f * 32 + 1], (HALF, 128))
+            rc = jnp.broadcast_to(row_cos[:, f * 32 : f * 32 + 1], (HALF, 128))
+            turns.append((col_sin[f : f + 1], col_cos[f : f + 1]))
+            c0h = c0s[f] * 0.5
             alternate = (1.0 - 4.0 * jnp.abs(c0h - jnp.floor(c0h))) * np.float32(1.0 / PIXELS)
             for c in range(2):
                 zr = lines[:64, c * 128 : c * 128 + 128]
@@ -598,7 +608,7 @@
             pupil = []
             for f in range(g, g + GROUP):
                 item = s * 4 + f
-                one0 = cosine(phases[:, f * 128 : f * 128 + 128] - quarter) * lens[0]
+                one0 = cosine(phases[:SIDE, f * 128 : f * 128 + 128] - quarter) * lens[0]
                 two0 = pltpu.roll(one0, 64, 1)
                 one1 = one0 * lens[1] + two0 * lens[2]
                 fields[item, 0] = two0
@@ -816,6 +826,22 @@
                     result[1, s // 2, s % 2, pl.ds(j * 8, 8), :] = -out[at + 8 : at + 16]
         result_copy().start()
 
+    def departures(it):
+        if nf > 1:
+            def field(s):
+                @pl.when(mine(s))
+                def _():
+                    if own < TILES:
+                        landed(sums.at[it, s, pl.ds(0, TILES - own)], rs_send.at[it, s])
+                    landed(parts.at[it, s // 2, pl.ds(0, nf - 1), :, pl.ds(0, 2)], ag_send.at[it, s // 2])
+
+                pl.when(jnp.logical_not(mine(s)))(lambda: landed(sums.at[it, s], rs_send.at[it, s]))
+
+            loop(0, FIELDS, field)
+            n1_copy(it, lax.rem(me, 2)).wait_send()
+        for inside, copy in halo_copies(it):
+            pl.when(inside)(copy.wait_send)
+
     def iteration(it):
         cf = coefs[...]
 
@@ -887,6 +913,7 @@
         smoothed = cf - step[0, 0] * smooth[0, 0] * laplace
         out = bend(jnp.concatenate([smoothed, grads], axis=0))
         pl.when(it == ITERS - 1)(write_object)
+        departures(it)
 
         if chips > 1:
             landed(norm2.at[it, pl.ds(0, chips - 1)], n2_recv.at[it])
@@ -897,24 +924,6 @@
         coefs[...] = smoothed - pace * grads
         store_bent(out[:ITEMS] - pace * out[ITEMS:])
 
-    def departures(it):
-        if nf > 1:
-            def field(s):
-                @pl.when(mine(s))
-                def _():
-                    if own < TILES:
-                        landed(sums.at[it, s, pl.ds(0, TILES - own)], rs_send.at[it, s])
-                    landed(parts.at[it, s // 2, pl.ds(0, nf - 1), :, pl.ds(0, 2)], ag_send.at[it, s // 2])
-
-                pl.when(jnp.logical_not(mine(s)))(lambda: landed(sums.at[it, s], rs_send.at[it, s]))
-
-            loop(0, FIELDS, field)
-            n1_copy(it, lax.rem(me, 2)).wait_send()
-        if chips > 1:
-            landed(norm2.at[it, pl.ds(0, chips - 1)], n2_send.at[it])
-        for inside, copy in halo_copies(it):
-            pl.when(inside)(copy.wait_send)
-
     loop(0, ITERS, iteration)
 
     for f in range(FRAMES):
@@ -922,7 +931,9 @@
             coefs_out[f, s // 2, pl.ds(s % 2, 1), :] = coefs[pl.ds(s * 4 + f, 1), pl.ds(0, MODES)]
 
     result_copy().wait()
-    loop(0, ITERS, departures)
+    if chips > 1:
+        for it in range(ITERS):
+            landed(norm2.at[it, pl.ds(0, chips - 1)], n2_send.at[it])
 
 
 def deliver(coefs, objects, coefs_out, object_out):

time: 65.3 us -> 64.8 us (level)
  no operation moved by 1% of the time
where the time goes in v7:
time: 64.8 us; the launch traced here: 64.6 us
  Pallas kernels  62 us (96%)
  between operations  2.58 us (4%)
    pallas_call x1, Pallas kernels, body(): pl.pallas_call(functools.partial(kernel, nf, nr, nc), out_shape=(jax.Shap...  60.6 us
    pallas_call x1, Pallas kernels, body(): pl.pallas_call(deliver, out_shape=tuple((jax.ShapeDtypeStruct(x.shape, x....  1.4 us

profile of v7, /device:TPU:1, one launch (start us, length us, event | category | flops | bytes accessed | tf_op | source)
XLA Modules:
  0.0 64.6 jit_solution(16971556927909617518)
XLA Ops:
  2.6 60.6 %shard_map.239 = (f32[4,2,2,36]{3,2,1,0:T(2,128)}, f32[2,2,2,8,128]{4,3,2,1,0:T(8,128)}) custom-call(bf16[4,2,2,2,128,128]{5,4,3,2,1,0:T(8,128)(2,1)} %images.1, s32[2,2,2,4]{3,2,1,0:T(2,128)} %bitcast.7, s32[2,2]{1,0:T(2,128)} %kinds.1, f32[4,2,2,36]{3,2,1,0:T(2,128)} %coefs_in.1, f32[1,1]{1,0:T(1,128)} %bitcast.4.step, f32[1,1]{1,0:T(1,128)} %bitcast.5.noise, ...), custom_call_target="tpu_custom_call" | custom-call | tf_op jit(solution)/shard_map/pallas_call | solution.py:984
  63.2 1.4 %shard_map.240 = (f32[4,2,2,36]{3,2,1,0:T(2,128)}, f32[2,2,2,8,128]{4,3,2,1,0:T(8,128)}) custom-call(f32[4,2,2,36]{3,2,1,0:T(2,128)} %get-tuple-element.4.coefs, f32[2,2,2,8,128]{4,3,2,1,0:T(8,128)} %get-tuple-element.5.objects), custom_call_target="tpu_custom_call" | custom-call | tf_op jit(solution)/shard_map/pallas_call | solution.py:1003

commit v8 on v7

--- a/solution.py
+++ b/solution.py
@@ -529,7 +529,7 @@
                 objs[it, s, tile, 0] = real / (power + n)
                 objs[it, s, tile, 1] = jnp.where(m064 & first, 0.0, imag / (other + n))
             at = pl.ds(k * own, own)
-            for j in sorted(range(1, nf), key=lambda j: -min(j // 4, 4 - j // 4) - j // 2 % 2):
+            for j in range(1, nf):
                 remote(
                     objs.at[it, s, at], objs.at[it, s, at],
                     ag_send.at[it, s // 2], ag_recv.at[it, s], {"frame": frames[j]},
@@ -849,11 +849,11 @@
             pl.when(it == 0)(lambda: data_field(s))
             forward(it, s)
 
-            first = (it == 0) & (s == 2)
+            first = (it == 0) & (s == 1)
             if npeers:
                 pl.when(first)(lambda: pl.semaphore_wait(barrier, npeers))
-            pl.when(first)(lambda: loop(0, 2, lambda s: send_field(it, s)))
-            pl.when((it > 0) | (s >= 2))(lambda: send_field(it, s))
+            pl.when(first)(lambda: loop(0, 1, lambda s: send_field(it, s)))
+            pl.when((it > 0) | (s >= 1))(lambda: send_field(it, s))
 
         def backward_step(s):
             wait_field(it, s)

time: 64.8 us -> 63.7 us (0.983)
  Pallas kernels: 62 us -> 60.9 us
    pallas_call x1, Pallas kernels: 60.6 us -> 59.5 us  [body(): pl.pallas_call(functools.partial(kernel, nf, nr, nc), out_shape=(jax.Shap...]
where the time goes in v8:
time: 63.7 us; the launch traced here: 63.5 us
  Pallas kernels  60.9 us (96%)
  between operations  2.58 us (4%)
    pallas_call x1, Pallas kernels, body(): pl.pallas_call(functools.partial(kernel, nf, nr, nc), out_shape=(jax.Shap...  59.5 us
    pallas_call x1, Pallas kernels, body(): pl.pallas_call(deliver, out_shape=tuple((jax.ShapeDtypeStruct(x.shape, x....  1.4 us

profile of v8, /device:TPU:1, one launch (start us, length us, event | category | flops | bytes accessed | tf_op | source)
XLA Modules:
  0.0 63.5 jit_solution(10286174468878285329)
XLA Ops:
  2.6 59.5 %shard_map.239 = (f32[4,2,2,36]{3,2,1,0:T(2,128)}, f32[2,2,2,8,128]{4,3,2,1,0:T(8,128)}) custom-call(bf16[4,2,2,2,128,128]{5,4,3,2,1,0:T(8,128)(2,1)} %images.1, s32[2,2,2,4]{3,2,1,0:T(2,128)} %bitcast.7, s32[2,2]{1,0:T(2,128)} %kinds.1, f32[4,2,2,36]{3,2,1,0:T(2,128)} %coefs_in.1, f32[1,1]{1,0:T(1,128)} %bitcast.4.step, f32[1,1]{1,0:T(1,128)} %bitcast.5.noise, ...), custom_call_target="tpu_custom_call" | custom-call | tf_op jit(solution)/shard_map/pallas_call | solution.py:984
  62.1 1.4 %shard_map.240 = (f32[4,2,2,36]{3,2,1,0:T(2,128)}, f32[2,2,2,8,128]{4,3,2,1,0:T(8,128)}) custom-call(f32[4,2,2,36]{3,2,1,0:T(2,128)} %get-tuple-element.4.coefs, f32[2,2,2,8,128]{4,3,2,1,0:T(8,128)} %get-tuple-element.5.objects), custom_call_target="tpu_custom_call" | custom-call | tf_op jit(solution)/shard_map/pallas_call | solution.py:1003
